TPU v7x, 32 devices: a whole 2x2x4 slice. The times are simulated.
32 devices in a mesh: wide: 16 (over z, y, x), narrow: 2 (over core).
Axes of the slice: x: 2, y: 2, z: 4, core: 2. Of those that a mesh axis runs over, the one named last changes fastest.
Arguments:
- queries: bfloat16 [4096, 2048], P(('wide', 'narrow')), may hold values from -6 to 6
- keys: bfloat16 [4096, 2048], P(('wide', 'narrow')), may hold values from -6 to 6
- values: bfloat16 [4096, 2048], P(('wide', 'narrow')), may hold values from -6 to 6
Outputs:
- attended: bfloat16 [4096, 2048], P(('wide', 'narrow'))
All inputs are finite; a program needn't handle non-finite values.
Results may differ from a plain program's by a relative error of at most 0.008.
Values sent between devices are 32-bit elements; how exact they have to be, the bound alone decides.
No kernel may reach another device: no remote copies, remote signals or barrier semaphores. Data moves between devices by JAX's collectives and lax.ppermute only.
A program may use at most 192 MiB of HBM per device.

v0:
```python
import jax
import jax.numpy as jnp
from jax import lax
from jax.sharding import PartitionSpec as P

HEADS = 16
HEAD_DIM = 128


def partner_2(block, axis, distance):
    count = lax.axis_size(axis)
    route = []
    for low in range(count):
        high = low | 1 << distance
        if high != low and high < count:
            route += [(low, high), (high, low)]
    return lax.ppermute(block, axis, route)


def carried_in(value, axis, combine, identity):
    count, mine = (lax.axis_size(axis), lax.axis_index(axis))
    everything = lax.all_gather(value, axis)
    start = jnp.broadcast_to(jnp.asarray(identity, value.dtype), value.shape)

    def step(k, before):
        reached = k < mine
        new = combine(before, everything[k])
        return jnp.where(reached, new, before)

    return lax.fori_loop(0, count, step, start)


def add_states(earlier, later):
    return earlier + later


def shards(queries, keys, values):
    tokens = queries.shape[0]
    q_heads = queries.reshape(tokens, HEADS, HEAD_DIM)
    k_heads = keys.reshape(tokens, HEADS, HEAD_DIM)
    v_heads = values.reshape(tokens, HEADS, HEAD_DIM)
    own_state = jnp.einsum("shd,she->hde", k_heads, v_heads, preferred_element_type=jnp.float32)
    empty = jnp.zeros_like(own_state)
    half_heads = HEADS // lax.axis_size("narrow")
    partner = partner_2(own_state, "narrow", 0)
    upper = lax.axis_index("narrow") == 1
    below = jnp.where(upper, partner, empty)
    whole_group = own_state + partner
    first_head = lax.axis_index("narrow") * half_heads
    group_state = lax.dynamic_slice_in_dim(whole_group, first_head, half_heads, 0)
    outer_part = carried_in(group_state, "wide", add_states, jnp.zeros_like(group_state))
    outer_part = lax.all_gather(outer_part, "narrow", axis=0, tiled=True)
    carry = outer_part + below
    rows = jnp.arange(tokens, dtype=jnp.int32)
    causal = rows[None, :, None] >= rows[None, None, :]
    scores = jnp.einsum("thd,shd->hts", q_heads, k_heads, preferred_element_type=jnp.float32)
    scores = jnp.where(causal, scores, 0.0).astype(jnp.bfloat16)
    local = jnp.einsum("hts,shd->thd", scores, v_heads, preferred_element_type=jnp.float32)
    carry_high = carry.astype(jnp.bfloat16)
    carry_low = (carry - carry_high.astype(jnp.float32)).astype(jnp.bfloat16)
    carried = jnp.einsum("thd,hde->the", q_heads, carry_high, preferred_element_type=jnp.float32)
    carried = carried + jnp.einsum(
        "thd,hde->the", q_heads, carry_low, preferred_element_type=jnp.float32
    )
    total = local + carried
    factor = lax.rsqrt(jnp.mean(total * total, axis=-1, keepdims=True) + 1e-05)
    return (total * factor).astype(jnp.bfloat16).reshape(tokens, HEADS * HEAD_DIM)


def solution(mesh):
    placed = (P(("wide", "narrow"), None), P(("wide", "narrow"), None), P(("wide", "narrow"), None))
    return jax.shard_map(
        shards, mesh=mesh, in_specs=placed, out_specs=P(("wide", "narrow"), None), check_vma=False
    )
```

profile of v0, /device:TPU:0, one launch (start us, length us, event | category | flops | bytes accessed | tf_op | source)
XLA Modules:
  0.0 168.2 jit_solution(9665410580218982297)
XLA Ops:
  6.5 1.4 copy.22
  7.9 1.3 fusion.5
  9.8 2.3 %collective-permute-done = f32[16,128,128]{2,1,0:T(8,128)S(1)} collective-permute-done((f32[16,128,128]{2,1,0:T(8,128)S(1)}, f32[16,128,128]{2,1,0:T(8,128)S(1)}, u32[]{:S(2)}, u32[]{:S(2)}) %collective-permute-start) | collective-permute-done | bytes 1048608 | tf_op jit(solution)/shard_map/ppermute | solution.py:17
  13.0 115.5 %all-gather.6.cloned.1.call-done = f32[128,128,128]{2,1,0:T(8,128)} async-done(((f32[8,128,128]{2,1,0:T(8,128)}), f32[128,128,128]{2,1,0:T(8,128)}) %all-gather.6.cloned.1.call-update) | async-done | bytes 8388624 | tf_op jit(solution)/shard_map/all_gather | solution.py:22
  128.5 20.0 %while.14 = (s32[]{:T(128)}, f32[8,128,128]{2,1,0:T(8,128)S(1)}, s32[]{:T(128)}, f32[16,8,128,128]{3,2,1,0:T(8,128)}, s32[]{:T(128)}, /*index=5*/s32[]{:T(128)}) while((s32[]{:T(128)}, f32[8,128,128]{2,1,0:T(8,128)S(1)}, s32[]{:T(128)}, f32[16,8,128,128]{3,2,1,0:T(8,128)}, s32[]{:T(128)}, /*index=5*/s32[]{:T(128)}) %tuple.40), condition=%wide.region_1.2_spmd.clone, body=%wide.region_0.1_spmd.clone.sunk | while | flops 393220 | bytes 1572957 | solution.py:30
  129.8 1.2 add_select_fusion.2
  131.0 1.2 add_select_fusion.2
  132.3 1.2 add_select_fusion.2
  133.5 1.2 add_select_fusion.2
  134.8 1.2 add_select_fusion.2
  136.0 1.2 add_select_fusion.2
  137.3 1.2 add_select_fusion.2
  138.5 1.2 add_select_fusion.2
  139.8 1.2 add_select_fusion.2
  141.0 1.2 add_select_fusion.2
  142.3 1.2 add_select_fusion.2
  143.6 1.2 add_select_fusion.2
  144.8 1.2 add_select_fusion.2
  146.1 1.2 add_select_fusion.2
  147.3 1.2 add_select_fusion.2
  149.4 1.7 %convolution_bitcast_fusion = f32[128,16,128]{0,2,1:T(8,128)S(1)} fusion(bf16[128,16,128]{0,2,1:T(8,128)(2,1)S(1)} %bitcast.49, pred[128,128]{1,0:T(8,128)(4,1)S(1)} %iota_compare_fusion, bf16[128,2048]{1,0:T(8,128)(2,1)} %param.7, bf16[128,2048]{1,0:T(8,128)(2,1)S(1)} %copy-done), kind=kOutput, calls=%fused_computation.5 | convolution fusion | flops 134742016 | bytes 2637824 | tf_op jit(solution)/shard_map/hts,shd->thd/dot_general | solution.py:58
  151.1 5.6 %all-gather.4.cloned.1.call-done = f32[16,128,128]{2,1,0:T(8,128)} async-done(((f32[8,128,128]{2,1,0:T(8,128)}), f32[16,128,128]{2,1,0:T(8,128)}) %all-gather.4.cloned.1.call-update) | async-done | bytes 1048592 | tf_op jit(solution)/shard_map/all_gather | solution.py:52
  156.7 1.7 %fusion.3 = f32[16,128,128]{2,1,0:T(8,128)S(1)} fusion(f32[16,128,128]{2,1,0:T(8,128)} %all-gather.4.cloned.1.call-done, f32[16,128,128]{2,1,0:T(8,128)S(1)} %collective-permute-done, pred[]{:T(512)S(6)} %eq.3, bf16[128,2048]{1,0:T(8,128)(2,1)S(1)} %copy-done), kind=kOutput, calls=%fused_computation.11 | convolution fusion | flops 68681728 | bytes 3670017 | tf_op jit(solution)/shard_map/thd,hde->the/dot_general | solution.py:62
  158.5 1.8 %multiply_reduce_fusion = (f32[128,16]{0,1:T(8,128)S(1)}, f32[128,16,128]{0,2,1:T(8,128)S(1)}) fusion(f32[128,16,128]{0,2,1:T(8,128)S(1)} %convolution_bitcast_fusion, f32[16,128,128]{2,1,0:T(8,128)S(1)} %fusion.3, f32[16,128,128]{2,1,0:T(8,128)} %all-gather.4.cloned.1.call-done, f32[16,128,128]{2,1,0:T(8,128)S(1)} %collective-permute-done, pred[]{:T(512)S(6)} %eq.3, ...), kind=kOutput, calls=%fused_computation.8 | convolution fusion | flops 68941824 | bytes 5775361 | tf_op jit(solution)/shard_map/thd,hde->the/dot_general | solution.py:61
  (16 shorter events, 4.6 us)
Async XLA Ops:
  6.5 142.9 %copy-start = (bf16[128,2048]{1,0:T(8,128)(2,1)S(1)}, bf16[128,2048]{1,0:T(8,128)(2,1)}, u32[]{:S(2)}) copy-start(bf16[128,2048]{1,0:T(8,128)(2,1)} %param.5) | copy-start | bytes 1572868
  6.5 122.0 %all-gather.6.cloned.1.call-start = ((), (), s32[]{:S(2)}) async-start(), calls=%async_computation.1 | async-start | bytes 8912896 | tf_op jit(solution)/shard_map/all_gather | solution.py:22
  9.3 2.8 %collective-permute-start = (f32[16,128,128]{2,1,0:T(8,128)S(1)}, f32[16,128,128]{2,1,0:T(8,128)S(1)}, u32[]{:S(2)}, u32[]{:S(2)}) collective-permute-start(f32[16,128,128]{2,1,0:T(8,128)S(1)} %fusion.5), channel_id=1, source_target_pairs={{0,1},{1,0},{2,3},{3,2},{4,5},{5,4},{6,7},{7,6},{8,9},{9,8},{10,11... | collective-permute-start | bytes 3145736 | tf_op jit(solution)/shard_map/ppermute | solution.py:17
  12.9 143.8 %all-gather.4.cloned.1.call-start = ((), (), s32[]{:S(2)}) async-start(), calls=%async_computation | async-start | bytes 1572864 | tf_op jit(solution)/shard_map/all_gather | solution.py:52
  148.5 0.8 copy-start.1
Sparse Core Ops, SparseCore 0:
  13.1 115.4 all-gather.5
  149.5 7.2 all-gather.3
where the time goes:
time: 169 us; the launch traced here: 168 us
  waiting for transfers between devices  124 us (73%)
  other arithmetic  20.6 us (12%)
  between operations  13.5 us (8%)
  matrix products  6.55 us (4%)
  local copies, waits for them, and re-layouts  3.17 us (2%)
    all_gather x1, waiting for transfers between devices, carried_in(): everything = lax.all_gather(value, axis)  116 us
    select_n x16, other arithmetic, step(): return jnp.where(reached, new, before)  19.6 us
    all_gather x1, waiting for transfers between devices, shards(): outer_part = lax.all_gather(outer_part, 'narrow', axis=0, tiled=True)  5.65 us
  transfers between devices with their start and end apart: 3, of which 3 were waited for; matrix products, arithmetic and copies ran while one was open for 1% of the time, Pallas kernels for 0%

commit v1 on v0

v1 whole, which is shorter than its diff:
```python
import jax
import jax.numpy as jnp
from jax import lax
from jax.experimental import pallas as pl
from jax.experimental.pallas import tpu as pltpu
from jax.sharding import PartitionSpec as P

HEADS = 16
HEAD_DIM = 128
VMEM = pl.BlockSpec(memory_space=pltpu.VMEM)
LIMIT = 40 * 1024 * 1024


def call(kernel, outs, args, flops=0):
    moved = sum(a.size * a.dtype.itemsize for a in args)
    return pl.pallas_call(
        kernel,
        out_shape=outs,
        in_specs=[VMEM] * len(args),
        out_specs=jax.tree.map(lambda _: VMEM, outs),
        compiler_params=pltpu.CompilerParams(vmem_limit_bytes=LIMIT),
        cost_estimate=pl.CostEstimate(flops=flops, bytes_accessed=moved, transcendentals=0),
    )(*args)


def f32(*shape):
    return jax.ShapeDtypeStruct(shape, jnp.float32)


def half_states(keys, values, half, count):
    def kernel(k_ref, v_ref, s_ref):
        first = half() * (count * HEAD_DIM)
        for h in range(count):
            cols = pl.ds(pl.multiple_of(first + h * HEAD_DIM, HEAD_DIM), HEAD_DIM)
            s_ref[h] = lax.dot_general(
                k_ref[:, cols], v_ref[:, cols], (((0,), (0,)), ((), ())), preferred_element_type=jnp.float32
            )

    tokens = keys.shape[0]
    return call(
        kernel, f32(count, HEAD_DIM, HEAD_DIM), (keys, values), 2 * count * tokens * HEAD_DIM * HEAD_DIM
    )


def local_part(queries, keys, values):
    tokens = queries.shape[0]

    def kernel(q_ref, k_ref, v_ref, o_ref):
        rows = lax.broadcasted_iota(jnp.int32, (tokens, tokens), 0)
        cols = lax.broadcasted_iota(jnp.int32, (tokens, tokens), 1)
        causal = rows >= cols
        for h in range(HEADS):
            c = slice(h * HEAD_DIM, (h + 1) * HEAD_DIM)
            scores = lax.dot_general(
                q_ref[:, c], k_ref[:, c], (((1,), (1,)), ((), ())), preferred_element_type=jnp.float32
            )
            scores = jnp.where(causal, scores, 0.0).astype(jnp.bfloat16)
            o_ref[:, c] = jnp.dot(scores, v_ref[:, c], preferred_element_type=jnp.float32)

    return call(
        kernel, f32(tokens, HEADS * HEAD_DIM), (queries, keys, values), 4 * HEADS * tokens * tokens * HEAD_DIM
    )


def finish(queries, local, own, other, below_own, below_other):
    tokens = queries.shape[0]
    count = own.shape[0]

    def kernel(q_ref, l_ref, a_ref, b_ref, ba_ref, bb_ref, o_ref):
        mine = lax.axis_index("narrow")
        upper = mine.astype(jnp.float32)
        for part, (c_ref, below_ref) in enumerate(((a_ref, ba_ref), (b_ref, bb_ref))):
            first = (mine if part == 0 else 1 - mine) * (count * HEAD_DIM)
            for h in range(count):
                cols = pl.ds(pl.multiple_of(first + h * HEAD_DIM, HEAD_DIM), HEAD_DIM)
                carry = c_ref[h] + below_ref[h] * upper
                high = carry.astype(jnp.bfloat16)
                low = (carry - high.astype(jnp.float32)).astype(jnp.bfloat16)
                q = q_ref[:, cols]
                total = (
                    l_ref[:, cols]
                    + jnp.dot(q, high, preferred_element_type=jnp.float32)
                    + jnp.dot(q, low, preferred_element_type=jnp.float32)
                )
                factor = lax.rsqrt(jnp.mean(total * total, axis=-1, keepdims=True) + 1e-05)
                o_ref[:, cols] = (total * factor).astype(jnp.bfloat16)

    return call(
        kernel,
        jax.ShapeDtypeStruct(queries.shape, jnp.bfloat16),
        (queries, local, own, other, below_own, below_other),
        4 * HEADS * tokens * HEAD_DIM * HEAD_DIM,
    )


def prefixes(states, own, group):
    def kernel(x_ref, p_ref, t_ref):
        run = jnp.zeros(x_ref.shape[1:], jnp.float32)
        for i in range(group):
            p_ref[i] = run
            run = run + x_ref[i]
        t_ref[...] = run

    return call(kernel, (f32(*states.shape), f32(*states.shape[1:])), (states,))


def swap_cores(block):
    return lax.ppermute(block, "narrow", [(0, 1), (1, 0)])


def shards(queries, keys, values):
    chips = lax.axis_size("wide")
    count = HEADS // lax.axis_size("narrow")
    group = count
    groups = chips // group
    me = lax.axis_index("narrow")

    given = half_states(keys, values, lambda: 1 - lax.axis_index("narrow"), count)
    got = swap_cores(given)
    kept = half_states(keys, values, lambda: lax.axis_index("narrow"), count)
    below_other = swap_cores(kept)
    chip = kept + got
    cubes = [[g * group + r for r in range(group)] for g in range(groups)]
    theirs = lax.all_to_all(chip, "wide", 0, 0, axis_index_groups=cubes, tiled=True)
    before, running = prefixes(theirs, None, group)
    where = lax.axis_index("wide") // group
    earlier = jnp.zeros_like(running)
    step = 1
    while step < groups:
        route = [(i, i ^ (step * group)) for i in range(chips)]
        seen = lax.ppermute(running, "wide", route)
        earlier = earlier + jnp.where((where & step) != 0, seen, 0.0)
        running = running + seen
        step *= 2
    local = local_part(queries, keys, values)
    outer = lax.all_to_all(before + earlier, "wide", 0, 0, axis_index_groups=cubes, tiled=True)
    outer_other = swap_cores(outer)
    return finish(queries, local, outer, outer_other, got, below_other)


def solution(mesh):
    placed = P(("wide", "narrow"), None)
    return jax.shard_map(
        shards, mesh=mesh, in_specs=(placed, placed, placed), out_specs=placed, check_vma=False
    )
```

time: 169 us -> 43.7 us (0.26)
  waiting for transfers between devices: 124 us -> 12.1 us
  other arithmetic: 20.6 us -> 0.9 us
  blocking collectives: 0 us -> 15.6 us
  between operations: 13.5 us -> 0.07 us
  matrix products: 6.55 us -> 0 us
  starting transfers between devices: 0.56 us -> 6.87 us
  Pallas kernels: 0 us -> 5.68 us
    all_gather x2 -> x0, waiting for transfers between devices: 121 us -> none  [the longest x1 116 us: carried_in(): everything = lax.all_gather(value, axis)]
    select_n x16 -> x1, other arithmetic: 19.6 us -> 0.01 us  [shards(): earlier = earlier + jnp.where(where & step != 0, seen, 0.0)]
    all_to_all x0 -> x1, blocking collectives: none -> 15.6 us  [shards(): lax.all_to_all(chip, 'wide', 0, 0, axis_index_groups=cubes, tiled=True)]
    all_to_all x0 -> x1, waiting for transfers between devices: none -> 7.53 us  [shards(): lax.all_to_all(before + earlier, 'wide', 0, 0, axis_index_groups=cubes, t...]
    dot_general x4 -> x0, matrix products: 6.55 us -> none  [the longest x1 1.77 us: shards(): jnp.einsum('thd,hde->the', q_heads, carry_high, preferred_element_type=jn...]
    pallas_call x0 -> x5, Pallas kernels: none -> 5.68 us  [call(): pl.pallas_call(kernel, out_shape=outs, in_specs=[VMEM] * len(args), out_s...]
    all_to_all x0 -> x1, starting transfers between devices: none -> 3.63 us  [shards(): lax.all_to_all(before + earlier, 'wide', 0, 0, axis_index_groups=cubes, t...]
    ppermute x1 -> x4, starting transfers between devices: 0.51 us -> 3.24 us  [the longest x1 2.65 us: shards(): seen = lax.ppermute(running, 'wide', route)]
  transfers between devices with their start and end apart: 3 -> 5, of which waited for: 3 -> 3; matrix products, arithmetic and copies ran while one was open for 1% -> 0% of each run, Pallas kernels for 0% -> 7%
where the time goes in v1:
time: 43.7 us; the launch traced here: 43.3 us
  blocking collectives  15.6 us (36%)
  waiting for transfers between devices  12.1 us (28%)
  starting transfers between devices  6.87 us (16%)
  Pallas kernels  5.68 us (13%)
  local copies, waits for them, and re-layouts  2.1 us (5%)
  other arithmetic  0.9 us (2%)
    all_to_all x1, blocking collectives, shards(): lax.all_to_all(chip, 'wide', 0, 0, axis_index_groups=cubes, tiled=True)  15.6 us
    all_to_all x1, waiting for transfers between devices, shards(): lax.all_to_all(before + earlier, 'wide', 0, 0, axis_index_groups=cubes, t...  7.53 us
    pallas_call x5, Pallas kernels, call(): pl.pallas_call(kernel, out_shape=outs, in_specs=[VMEM] * len(args), out_s...  5.68 us
    all_to_all x1, starting transfers between devices, shards(): lax.all_to_all(before + earlier, 'wide', 0, 0, axis_index_groups=cubes, t...  3.63 us
    ppermute x1, waiting for transfers between devices, shards(): seen = lax.ppermute(running, 'wide', route)  3.28 us
    ppermute x1, starting transfers between devices, shards(): seen = lax.ppermute(running, 'wide', route)  2.65 us
    unnamed x10, local copies, waits for them, and re-layouts  2.1 us
    ppermute x3, waiting for transfers between devices, swap_cores(): return lax.ppermute(block, 'narrow', [(0, 1), (1, 0)])  1.25 us
  transfers between devices with their start and end apart: 5, of which 3 were waited for; matrix products, arithmetic and copies ran while one was open for 0% of the time, Pallas kernels for 7%

profile of v1, /device:TPU:0, one launch (start us, length us, event | category | flops | bytes accessed | tf_op | source)
XLA Modules:
  0.0 43.3 jit_solution(2614229433021895183)
XLA Ops:
  0.0 0.0 copy-start
  0.0 1.0 %copy-done = bf16[128,2048]{1,0:T(8,128)(2,1)S(1)} copy-done((bf16[128,2048]{1,0:T(8,128)(2,1)S(1)}, bf16[128,2048]{1,0:T(8,128)(2,1)}, u32[]{:S(2)}) %copy-start) | copy-done | bytes 524312
  1.0 1.0 %copy-done.2 = bf16[128,2048]{1,0:T(8,128)(2,1)S(1)} copy-done((bf16[128,2048]{1,0:T(8,128)(2,1)S(1)}, bf16[128,2048]{1,0:T(8,128)(2,1)}, u32[]{:S(2)}) %copy-start.2) | copy-done | bytes 524312
  2.1 0.3 shard_map.39
  2.4 0.5 %collective-permute-start = (f32[8,128,128]{2,1,0:T(8,128)S(1)}, f32[8,128,128]{2,1,0:T(8,128)S(1)}, u32[]{:S(2)}, u32[]{:S(2)}) collective-permute-start(f32[8,128,128]{2,1,0:T(8,128)S(1)} %shard_map.39), channel_id=1, source_target_pairs={{0,1},{1,0},{2,3},{3,2},{4,5},{5,4},{6,7},{7,6},{8,9},{9,8},{10,11... | collective-permute-start | bytes 1572872 | tf_op jit(solution)/shard_map/ppermute | solution.py:108
  2.9 0.3 shard_map.38
  3.2 1.2 %collective-permute-done.ba_ref = f32[8,128,128]{2,1,0:T(8,128)S(1)} collective-permute-done((f32[8,128,128]{2,1,0:T(8,128)S(1)}, f32[8,128,128]{2,1,0:T(8,128)S(1)}, u32[]{:S(2)}, u32[]{:S(2)}) %collective-permute-start) | collective-permute-done | bytes 524320 | tf_op jit(solution)/shard_map/ppermute | solution.py:108
  4.4 0.1 add.12
  4.5 15.6 %all_to_all.10.x_ref = f32[8,128,128]{2,1,0:T(8,128)S(1)} all-to-all(f32[8,128,128]{2,1,0:T(8,128)S(1)} %add.12), channel_id=1, replica_groups={{0,2,4,6,8,10,12,14},{16,18,20,22,24,26,28,30},{1,3,5,7,9,11,13,15},{17..., dimensions={0} | all-to-all | bytes 1048576 | tf_op jit(solution)/shard_map/all_to_all | solution.py:124
  20.1 2.7 %collective-permute-start.1 = (f32[128,128]{1,0:T(8,128)S(1)}, f32[128,128]{1,0:T(8,128)S(1)}, u32[]{:S(2)}, u32[]{:S(2)}) collective-permute-start(f32[128,128]{1,0:T(8,128)S(1)} %get-tuple-element.8), channel_id=1, source_target_pairs={{0,16},{2,18},{4,20},{6,22},{8,24},{10,26},{12,28},{14,30},{16,0},... | collective-permute-start | bytes 196616 | tf_op jit(solution)/shard_map/ppermute | solution.py:131
  22.8 3.3 %collective-permute-done.1 = f32[128,128]{1,0:T(8,128)S(1)} collective-permute-done((f32[128,128]{1,0:T(8,128)S(1)}, f32[128,128]{1,0:T(8,128)S(1)}, u32[]{:S(2)}, u32[]{:S(2)}) %collective-permute-start.1) | collective-permute-done | bytes 65568 | tf_op jit(solution)/shard_map/ppermute | solution.py:131
  26.1 0.0 copy-start.4
  26.1 0.8 %broadcast_add_fusion = f32[8,128,128]{2,1,0:T(8,128)} fusion(f32[8,128,128]{2,1,0:T(8,128)S(1)} %get-tuple-element.7, f32[128,128]{1,0:T(8,128)S(1)} %broadcast_select_fusion), kind=kLoop, calls=%fused_computation | loop fusion | flops 131072 | bytes 1114112 | tf_op jit(solution)/shard_map/add | solution.py:136
  26.9 3.6 %all-to-all-start.1 = ((f32[8,128,128]{2,1,0:T(8,128)}), f32[8,128,128]{2,1,0:T(8,128)S(1)}, u32[]{:S(2)}, u32[]{:S(2)}) async-start(f32[8,128,128]{2,1,0:T(8,128)} %broadcast_add_fusion), calls=%async_computation.1 | async-start | bytes 1048576 | tf_op jit(solution)/shard_map/all_to_all | solution.py:136
  30.6 0.1 collective-permute-start.3
  30.7 7.5 %all-to-all-done.1.a_ref = f32[8,128,128]{2,1,0:T(8,128)S(1)} async-done(((f32[8,128,128]{2,1,0:T(8,128)}), f32[8,128,128]{2,1,0:T(8,128)S(1)}, u32[]{:S(2)}, u32[]{:S(2)}) %all-to-all-start.1) | async-done | bytes 524320 | tf_op jit(solution)/shard_map/all_to_all | solution.py:136
  38.2 0.0 collective-permute-start.2
  38.2 0.0 copy-done.4
  38.2 0.0 copy-done.1
  38.2 0.0 copy-done.3
  38.2 2.6 %shard_map.37.l_ref = f32[128,2048]{1,0:T(8,128)S(1)} custom-call(bf16[128,2048]{1,0:T(8,128)(2,1)S(1)} %copy-done.4, bf16[128,2048]{1,0:T(8,128)(2,1)S(1)} %copy-done.1, bf16[128,2048]{1,0:T(8,128)(2,1)S(1)} %copy-done.3), custom_call_target="tpu_custom_call" | custom-call | flops 134217728 | bytes 1572864 | tf_op jit(solution)/shard_map/pallas_call | solution.py:16
  40.8 0.0 collective-permute-done.3.bb_ref
  40.8 0.0 collective-permute-done.2.b_ref
  40.8 2.5 %shard_map.41 = bf16[128,2048]{1,0:T(8,128)(2,1)} custom-call(bf16[128,2048]{1,0:T(8,128)(2,1)S(1)} %copy-done.4, f32[128,2048]{1,0:T(8,128)S(1)} %shard_map.37.l_ref, f32[8,128,128]{2,1,0:T(8,128)S(1)} %all-to-all-done.1.a_ref, f32[8,128,128]{2,1,0:T(8,128)S(1)} %collective-permute-done.2.b_ref, f32[8,128,128]{2,1,0:T(8,128)S(1)} %collective-permute-done.ba_ref, ...), custom_call_target="tpu_custom_call" | custom-call | flops 134217728 | bytes 3670016 | tf_op jit(solution)/shard_map/pallas_call | solution.py:16
  (5 shorter events, 0.1 us)
Async XLA Ops:
  0.0 1.0 %copy-start = (bf16[128,2048]{1,0:T(8,128)(2,1)S(1)}, bf16[128,2048]{1,0:T(8,128)(2,1)}, u32[]{:S(2)}) copy-start(bf16[128,2048]{1,0:T(8,128)(2,1)} %k_ref.5) | copy-start | bytes 1572868
  1.0 1.0 %copy-start.2 = (bf16[128,2048]{1,0:T(8,128)(2,1)S(1)}, bf16[128,2048]{1,0:T(8,128)(2,1)}, u32[]{:S(2)}) copy-start(bf16[128,2048]{1,0:T(8,128)(2,1)} %v_ref.5) | copy-start | bytes 1572868
  2.4 2.1 %collective-permute-start = (f32[8,128,128]{2,1,0:T(8,128)S(1)}, f32[8,128,128]{2,1,0:T(8,128)S(1)}, u32[]{:S(2)}, u32[]{:S(2)}) collective-permute-start(f32[8,128,128]{2,1,0:T(8,128)S(1)} %shard_map.39), channel_id=1, source_target_pairs={{0,1},{1,0},{2,3},{3,2},{4,5},{5,4},{6,7},{7,6},{8,9},{9,8},{10,11... | collective-permute-start | bytes 1572872 | tf_op jit(solution)/shard_map/ppermute | solution.py:108
  20.1 5.9 %collective-permute-start.1 = (f32[128,128]{1,0:T(8,128)S(1)}, f32[128,128]{1,0:T(8,128)S(1)}, u32[]{:S(2)}, u32[]{:S(2)}) collective-permute-start(f32[128,128]{1,0:T(8,128)S(1)} %get-tuple-element.8), channel_id=1, source_target_pairs={{0,16},{2,18},{4,20},{6,22},{8,24},{10,26},{12,28},{14,30},{16,0},... | collective-permute-start | bytes 196616 | tf_op jit(solution)/shard_map/ppermute | solution.py:131
  26.1 12.1 %copy-start.4 = (bf16[128,2048]{1,0:T(8,128)(2,1)S(1)}, bf16[128,2048]{1,0:T(8,128)(2,1)}, u32[]{:S(2)}) copy-start(bf16[128,2048]{1,0:T(8,128)(2,1)} %q_ref.3) | copy-start | bytes 1572868
  26.9 11.3 %copy-start.1 = (bf16[128,2048]{1,0:T(8,128)(2,1)S(1)}, bf16[128,2048]{1,0:T(8,128)(2,1)}, u32[]{:S(2)}) copy-start(bf16[128,2048]{1,0:T(8,128)(2,1)} %k_ref.5) | copy-start | bytes 1572868
  26.9 11.3 %copy-start.3 = (bf16[128,2048]{1,0:T(8,128)(2,1)S(1)}, bf16[128,2048]{1,0:T(8,128)(2,1)}, u32[]{:S(2)}) copy-start(bf16[128,2048]{1,0:T(8,128)(2,1)} %v_ref.5) | copy-start | bytes 1572868
  26.9 11.2 %all-to-all-start.1 = ((f32[8,128,128]{2,1,0:T(8,128)}), f32[8,128,128]{2,1,0:T(8,128)S(1)}, u32[]{:S(2)}, u32[]{:S(2)}) async-start(f32[8,128,128]{2,1,0:T(8,128)} %broadcast_add_fusion), calls=%async_computation.1 | async-start | bytes 1048576 | tf_op jit(solution)/shard_map/all_to_all | solution.py:136
  30.6 10.2 %collective-permute-start.3 = (f32[8,128,128]{2,1,0:T(8,128)S(1)}, f32[8,128,128]{2,1,0:T(8,128)}, u32[]{:S(2)}, u32[]{:S(2)}) collective-permute-start(f32[8,128,128]{2,1,0:T(8,128)S(1)} %shard_map.38), channel_id=1, source_target_pairs={{0,1},{1,0},{2,3},{3,2},{4,5},{5,4},{6,7},{7,6},{8,9},{9,8},{10,11... | collective-permute-start | bytes 1572872 | tf_op jit(solution)/shard_map/ppermute | solution.py:108
  38.2 2.6 %collective-permute-start.2 = (f32[8,128,128]{2,1,0:T(8,128)S(1)}, f32[8,128,128]{2,1,0:T(8,128)S(1)}, u32[]{:S(2)}, u32[]{:S(2)}) collective-permute-start(f32[8,128,128]{2,1,0:T(8,128)S(1)} %all-to-all-done.1.a_ref), channel_id=1, source_target_pairs={{0,1},{1,0},{2,3},{3,2},{4,5},{5,4},{6,7},{7,6},{8,9},{9,8},{10,11... | collective-permute-start | bytes 1572872 | tf_op jit(solution)/shard_map/ppermute | solution.py:108

commit v2 on v1

v2 whole, which is shorter than its diff:
```python
import jax
import jax.numpy as jnp
from jax import lax
from jax.experimental import pallas as pl
from jax.experimental.pallas import tpu as pltpu
from jax.sharding import PartitionSpec as P

HEADS = 16
HEAD_DIM = 128
VMEM = pl.BlockSpec(memory_space=pltpu.VMEM)
HBM = pl.BlockSpec(memory_space=pltpu.HBM)
LIMIT = 8 * 1024 * 1024


def call(kernel, outs, args, flops=0, ins=None, out_specs=None, scratch=()):
    moved = sum(a.size * a.dtype.itemsize for a in args)
    return pl.pallas_call(
        kernel,
        out_shape=outs,
        in_specs=ins or [VMEM] * len(args),
        out_specs=out_specs or jax.tree.map(lambda _: VMEM, outs),
        scratch_shapes=scratch,
        compiler_params=pltpu.CompilerParams(vmem_limit_bytes=LIMIT),
        cost_estimate=pl.CostEstimate(flops=flops, bytes_accessed=moved, transcendentals=0),
    )(*args)


def f32(*shape):
    return jax.ShapeDtypeStruct(shape, jnp.float32)


def head(h, first=0):
    return pl.ds(pl.multiple_of(first + h * HEAD_DIM, HEAD_DIM), HEAD_DIM)


def half_states(keys, values, other, count, pieces=2):
    tokens = keys.shape[0]
    each = count // pieces
    width = each * HEAD_DIM

    def kernel(k_hbm, v_hbm, s_ref, k_ref, v_ref, sems):
        mine = lax.axis_index("narrow")
        first = (1 - mine if other else mine) * (count * HEAD_DIM)
        copies = []
        for p in range(pieces):
            cols = pl.ds(pl.multiple_of(first + p * width, width), width)
            for i, (src, dst) in enumerate(((k_hbm, k_ref), (v_hbm, v_ref))):
                copy = pltpu.make_async_copy(
                    src.at[:, cols], dst.at[:, p * width : (p + 1) * width], sems.at[p, i]
                )
                copy.start()
                copies.append(copy)
        for p in range(pieces):
            copies[2 * p].wait()
            copies[2 * p + 1].wait()
            for h in range(p * each, (p + 1) * each):
                cols = slice(h * HEAD_DIM, (h + 1) * HEAD_DIM)
                s_ref[h] = lax.dot_general(
                    k_ref[:, cols], v_ref[:, cols], (((0,), (0,)), ((), ())), preferred_element_type=jnp.float32
                )

    return call(
        kernel,
        f32(count, HEAD_DIM, HEAD_DIM),
        (pltpu.with_memory_space_constraint(keys, pltpu.HBM), pltpu.with_memory_space_constraint(values, pltpu.HBM)),
        2 * count * tokens * HEAD_DIM * HEAD_DIM,
        ins=[HBM, HBM],
        scratch=[
            pltpu.VMEM((tokens, count * HEAD_DIM), keys.dtype),
            pltpu.VMEM((tokens, count * HEAD_DIM), values.dtype),
            pltpu.SemaphoreType.DMA((pieces, 2)),
        ],
    )


def local_part(queries, keys, values):
    tokens = queries.shape[0]

    def kernel(q_ref, k_ref, v_ref, o_ref):
        rows = lax.broadcasted_iota(jnp.int32, (tokens, tokens), 0)
        cols = lax.broadcasted_iota(jnp.int32, (tokens, tokens), 1)
        causal = rows >= cols
        for h in range(HEADS):
            c = slice(h * HEAD_DIM, (h + 1) * HEAD_DIM)
            scores = lax.dot_general(
                q_ref[:, c], k_ref[:, c], (((1,), (1,)), ((), ())), preferred_element_type=jnp.float32
            )
            scores = jnp.where(causal, scores, 0.0).astype(jnp.bfloat16)
            o_ref[:, c] = jnp.dot(scores, v_ref[:, c], preferred_element_type=jnp.float32)

    return call(
        kernel, f32(tokens, HEADS * HEAD_DIM), (queries, keys, values), 4 * HEADS * tokens * tokens * HEAD_DIM
    )


def attended(q, local, carry):
    high = carry.astype(jnp.bfloat16)
    low = (carry - high.astype(jnp.float32)).astype(jnp.bfloat16)
    total = local + jnp.dot(
        jnp.concatenate([q, q], axis=1), jnp.concatenate([high, low], axis=0), preferred_element_type=jnp.float32
    )
    factor = lax.rsqrt(jnp.mean(total * total, axis=-1, keepdims=True) + 1e-05)
    return (total * factor).astype(jnp.bfloat16)


def finish_own(queries, local, outer, got):
    tokens = queries.shape[0]
    count = outer.shape[0]

    def kernel(q_ref, l_ref, c_ref, g_ref, o_ref):
        mine = lax.axis_index("narrow")
        for h in range(count):
            cols = head(h, mine * (count * HEAD_DIM))
            carry = c_ref[h] + jnp.where(mine == 1, g_ref[h], 0.0)
            o_ref[:, h * HEAD_DIM : (h + 1) * HEAD_DIM] = attended(q_ref[:, cols], l_ref[:, cols], carry)

    return call(
        kernel,
        jax.ShapeDtypeStruct((tokens, count * HEAD_DIM), jnp.bfloat16),
        (queries, local, outer, got),
        4 * count * tokens * HEAD_DIM * HEAD_DIM,
    )


def finish_other(queries, local, carry, done, pieces=2):
    tokens = queries.shape[0]
    count = carry.shape[0]
    each = count // pieces
    width = each * HEAD_DIM

    def kernel(q_ref, l_ref, c_ref, d_ref, o_hbm, y_ref, sems):
        mine = lax.axis_index("narrow")
        half = count * HEAD_DIM
        copies = [
            pltpu.make_async_copy(d_ref, o_hbm.at[:, pl.ds(pl.multiple_of(mine * half, half), half)], sems.at[pieces])
        ]
        copies[0].start()
        first = (1 - mine) * half
        for p in range(pieces):
            for h in range(p * each, (p + 1) * each):
                cols = head(h, first)
                y_ref[:, h * HEAD_DIM : (h + 1) * HEAD_DIM] = attended(q_ref[:, cols], l_ref[:, cols], c_ref[h])
            copy = pltpu.make_async_copy(
                y_ref.at[:, p * width : (p + 1) * width],
                o_hbm.at[:, pl.ds(pl.multiple_of(first + p * width, width), width)],
                sems.at[p],
            )
            copy.start()
            copies.append(copy)
        for copy in copies:
            copy.wait()

    return call(
        kernel,
        jax.ShapeDtypeStruct(queries.shape, jnp.bfloat16),
        (queries, local, carry, done),
        4 * count * tokens * HEAD_DIM * HEAD_DIM,
        out_specs=HBM,
        scratch=[
            pltpu.VMEM((tokens, count * HEAD_DIM), jnp.bfloat16),
            pltpu.SemaphoreType.DMA((pieces + 1,)),
        ],
    )


def sum_of(states):
    def kernel(x_ref, t_ref):
        run = x_ref[0]
        for i in range(1, states.shape[0]):
            run = run + x_ref[i]
        t_ref[...] = run

    return call(kernel, f32(*states.shape[1:]), (states,))


def prefixes(states, start):
    def kernel(x_ref, s_ref, p_ref):
        run = s_ref[...]
        for i in range(states.shape[0]):
            p_ref[i] = run
            if i + 1 < states.shape[0]:
                run = run + x_ref[i]

    return call(kernel, f32(*states.shape), (states, start))


def add_lower(outer, kept):
    def kernel(a_ref, b_ref, o_ref):
        lower = lax.axis_index("narrow") == 0
        for h in range(outer.shape[0]):
            o_ref[h] = a_ref[h] + jnp.where(lower, b_ref[h], 0.0)

    return call(kernel, f32(*outer.shape), (outer, kept))


def swap_cores(block):
    return lax.ppermute(block, "narrow", [(0, 1), (1, 0)])


def shards(queries, keys, values):
    chips = lax.axis_size("wide")
    count = HEADS // lax.axis_size("narrow")
    group = count
    groups = chips // group
    cubes = [[g * group + r for r in range(group)] for g in range(groups)]

    given = half_states(keys, values, True, count)
    got = swap_cores(given)
    kept = half_states(keys, values, False, count)
    chip = kept + got
    theirs = lax.all_to_all(chip, "wide", 0, 0, axis_index_groups=cubes, tiled=True)

    cube = lax.axis_index("wide") // group
    running = sum_of(theirs)
    later_q, _ = lax.optimization_barrier((queries, running))
    local = local_part(later_q, keys, values)
    earlier = None
    step = 1
    while step < groups:
        seen = lax.ppermute(running, "wide", [(i, i ^ (step * group)) for i in range(chips)])
        lower = jnp.where((cube & step) != 0, seen, 0.0)
        earlier = lower if earlier is None else earlier + lower
        running = running + seen
        step *= 2
    earlier, local = lax.optimization_barrier((earlier, local))
    outer = lax.all_to_all(prefixes(theirs, earlier), "wide", 0, 0, axis_index_groups=cubes, tiled=True)
    other = swap_cores(add_lower(outer, kept))
    own = finish_own(queries, local, outer, got)
    return finish_other(queries, local, other, own)


def solution(mesh):
    placed = P(("wide", "narrow"), None)
    return jax.shard_map(
        shards, mesh=mesh, in_specs=(placed, placed, placed), out_specs=placed, check_vma=False
    )
```

time: 43.7 us -> 39.3 us (0.90)
  blocking collectives: 15.6 us -> 26.4 us
  waiting for transfers between devices: 12.1 us -> 2.28 us
  starting transfers between devices: 6.87 us -> 3.24 us
  local copies, waits for them, and re-layouts: 2.1 us -> 0.02 us
  Pallas kernels: 5.68 us -> 7.04 us
  other arithmetic: 0.9 us -> 0.06 us
    all_to_all x0 -> x1, blocking collectives: none -> 10.6 us  [shards(): lax.all_to_all(prefixes(theirs, earlier), 'wide', 0, 0, axis_index_groups...]
    all_to_all x1 -> x0, waiting for transfers between devices: 7.53 us -> none  [shards(): lax.all_to_all(before + earlier, 'wide', 0, 0, axis_index_groups=cubes, t...]
    all_to_all x1 -> x0, starting transfers between devices: 3.63 us -> none  [shards(): lax.all_to_all(before + earlier, 'wide', 0, 0, axis_index_groups=cubes, t...]
    ppermute x1, waiting for transfers between devices: 3.28 us -> 0.7 us  [shards(): lax.ppermute(running, 'wide', [(i, i ^ step * group) for i in range(chips)])]
    unnamed x10 -> x6, local copies, waits for them, and re-layouts: 2.1 us -> 0.02 us
    pallas_call x5 -> x8, Pallas kernels: 5.68 us -> 7.04 us  [call(): pl.pallas_call(kernel, out_shape=outs, in_specs=ins or [VMEM] * len(args)...]
    add x1 -> x0, other arithmetic: 0.83 us -> none  [shards(): before + earlier]
    ppermute x3 -> x2, waiting for transfers between devices: 1.25 us -> 1.59 us  [swap_cores(): return lax.ppermute(block, 'narrow', [(0, 1), (1, 0)])]
  transfers between devices with their start and end apart: 5 -> 3, of which waited for: 3 -> 3; matrix products, arithmetic and copies ran while one was open for 0% -> 0% of each run, Pallas kernels for 7% -> 11%
where the time goes in v2:
time: 39.3 us; the launch traced here: 39.1 us
  blocking collectives  26.4 us (67%)
  Pallas kernels  7.04 us (18%)
  starting transfers between devices  3.24 us (8%)
  waiting for transfers between devices  2.28 us (6%)
    all_to_all x1, blocking collectives, shards(): lax.all_to_all(chip, 'wide', 0, 0, axis_index_groups=cubes, tiled=True)  15.8 us
    all_to_all x1, blocking collectives, shards(): lax.all_to_all(prefixes(theirs, earlier), 'wide', 0, 0, axis_index_groups...  10.6 us
    pallas_call x8, Pallas kernels, call(): pl.pallas_call(kernel, out_shape=outs, in_specs=ins or [VMEM] * len(args)...  7.04 us
    ppermute x1, starting transfers between devices, shards(): lax.ppermute(running, 'wide', [(i, i ^ step * group) for i in range(chips)])  2.65 us
    ppermute x2, waiting for transfers between devices, swap_cores(): return lax.ppermute(block, 'narrow', [(0, 1), (1, 0)])  1.59 us
  transfers between devices with their start and end apart: 3, of which 3 were waited for; matrix products, arithmetic and copies ran while one was open for 0% of the time, Pallas kernels for 11%

profile of v2, /device:TPU:0, one launch (start us, length us, event | category | flops | bytes accessed | tf_op | source)
XLA Modules:
  0.0 39.1 jit_solution(5685664995121574462)
XLA Ops:
  0.0 1.4 %shard_map.38 = f32[8,128,128]{2,1,0:T(8,128)S(1)} custom-call(bf16[128,2048]{1,0:T(8,128)(2,1)} %k_ref.1, bf16[128,2048]{1,0:T(8,128)(2,1)} %v_ref.1), custom_call_target="tpu_custom_call" | custom-call | flops 33554432 | bytes 1048576 | tf_op jit(solution)/shard_map/pallas_call | solution.py:17
  1.4 0.5 %collective-permute-start = (f32[8,128,128]{2,1,0:T(8,128)S(1)}, f32[8,128,128]{2,1,0:T(8,128)S(1)}, u32[]{:S(2)}, u32[]{:S(2)}) collective-permute-start(f32[8,128,128]{2,1,0:T(8,128)S(1)} %shard_map.38), channel_id=1, source_target_pairs={{0,1},{1,0},{2,3},{3,2},{4,5},{5,4},{6,7},{7,6},{8,9},{9,8},{10,11... | collective-permute-start | bytes 1572872 | tf_op jit(solution)/shard_map/ppermute | solution.py:197
  2.0 1.4 %shard_map.37.b_ref = f32[8,128,128]{2,1,0:T(8,128)S(1)} custom-call(bf16[128,2048]{1,0:T(8,128)(2,1)} %k_ref.1, bf16[128,2048]{1,0:T(8,128)(2,1)} %v_ref.1), custom_call_target="tpu_custom_call" | custom-call | flops 33554432 | bytes 1048576 | tf_op jit(solution)/shard_map/pallas_call | solution.py:17
  3.4 0.1 collective-permute-done.g_ref
  3.5 0.1 add.4
  3.6 0.0 copy-start.1
  3.6 0.0 copy-start.2
  3.6 15.8 %all_to_all.10.x_ref = f32[8,128,128]{2,1,0:T(8,128)S(1)} all-to-all(f32[8,128,128]{2,1,0:T(8,128)S(1)} %add.4), channel_id=1, replica_groups={{0,2,4,6,8,10,12,14},{16,18,20,22,24,26,28,30},{1,3,5,7,9,11,13,15},{17..., dimensions={0} | all-to-all | bytes 1048576 | tf_op jit(solution)/shard_map/all_to_all | solution.py:211
  19.3 0.0 copy-start
  19.4 2.7 %collective-permute-start.1 = (f32[128,128]{1,0:T(8,128)S(1)}, f32[128,128]{1,0:T(8,128)S(1)}, u32[]{:S(2)}, u32[]{:S(2)}) collective-permute-start(f32[128,128]{1,0:T(8,128)S(1)} %shard_map.39), channel_id=1, source_target_pairs={{0,16},{2,18},{4,20},{6,22},{8,24},{10,26},{12,28},{14,30},{16,0},... | collective-permute-start | bytes 196616 | tf_op jit(solution)/shard_map/ppermute | solution.py:220
  22.0 0.0 copy-done.1
  22.0 0.0 copy-done.2
  22.0 0.0 copy-done
  22.0 2.6 %shard_map.40.l_ref = f32[128,2048]{1,0:T(8,128)S(1)} custom-call(bf16[128,2048]{1,0:T(8,128)(2,1)S(1)} %copy-done.2, bf16[128,2048]{1,0:T(8,128)(2,1)S(1)} %copy-done, bf16[128,2048]{1,0:T(8,128)(2,1)S(1)} %copy-done.1), custom_call_target="tpu_custom_call" | custom-call | flops 134217728 | bytes 1572864 | tf_op jit(solution)/shard_map/pallas_call | solution.py:17
  24.6 0.7 %collective-permute-done.1 = f32[128,128]{1,0:T(8,128)S(1)} collective-permute-done((f32[128,128]{1,0:T(8,128)S(1)}, f32[128,128]{1,0:T(8,128)S(1)}, u32[]{:S(2)}, u32[]{:S(2)}) %collective-permute-start.1) | collective-permute-done | bytes 65568 | tf_op jit(solution)/shard_map/ppermute | solution.py:220
  25.4 10.6 %all_to_all.11.a_ref.c_ref = f32[8,128,128]{2,1,0:T(8,128)S(1)} all-to-all(f32[8,128,128]{2,1,0:T(8,128)S(1)} %shard_map.41), channel_id=1, replica_groups={{0,2,4,6,8,10,12,14},{16,18,20,22,24,26,28,30},{1,3,5,7,9,11,13,15},{17..., dimensions={0} | all-to-all | bytes 1048576 | tf_op jit(solution)/shard_map/all_to_all | solution.py:226
  36.0 0.1 shard_map.42
  36.1 0.1 collective-permute-start.2
  36.1 0.4 %shard_map.43.d_ref = bf16[128,1024]{1,0:T(8,128)(2,1)S(1)} custom-call(bf16[128,2048]{1,0:T(8,128)(2,1)S(1)} %copy-done.2, f32[128,2048]{1,0:T(8,128)S(1)} %shard_map.40.l_ref, f32[8,128,128]{2,1,0:T(8,128)S(1)} %all_to_all.11.a_ref.c_ref, f32[8,128,128]{2,1,0:T(8,128)S(1)} %collective-permute-done.g_ref), custom_call_target="tpu_custom_call" | custom-call | flops 67108864 | bytes 2621440 | tf_op jit(solution)/shard_map/pallas_call | solution.py:17
  36.5 1.5 %collective-permute-done.2.c_ref = f32[8,128,128]{2,1,0:T(8,128)S(1)} collective-permute-done((f32[8,128,128]{2,1,0:T(8,128)S(1)}, f32[8,128,128]{2,1,0:T(8,128)S(1)}, u32[]{:S(2)}, u32[]{:S(2)}) %collective-permute-start.2) | collective-permute-done | bytes 524320 | tf_op jit(solution)/shard_map/ppermute | solution.py:197
  38.0 1.1 %shard_map.44 = bf16[128,2048]{1,0:T(8,128)(2,1)} custom-call(bf16[128,2048]{1,0:T(8,128)(2,1)S(1)} %copy-done.2, f32[128,2048]{1,0:T(8,128)S(1)} %shard_map.40.l_ref, f32[8,128,128]{2,1,0:T(8,128)S(1)} %collective-permute-done.2.c_ref, bf16[128,1024]{1,0:T(8,128)(2,1)S(1)} %shard_map.43.d_ref), custom_call_target="tpu_custom_call" | custom-call | flops 67108864 | bytes 2359296 | tf_op jit(solution)/shard_map/pallas_call | solution.py:17
  (3 shorter events, 0.1 us)
Async XLA Ops:
  1.4 2.1 %collective-permute-start = (f32[8,128,128]{2,1,0:T(8,128)S(1)}, f32[8,128,128]{2,1,0:T(8,128)S(1)}, u32[]{:S(2)}, u32[]{:S(2)}) collective-permute-start(f32[8,128,128]{2,1,0:T(8,128)S(1)} %shard_map.38), channel_id=1, source_target_pairs={{0,1},{1,0},{2,3},{3,2},{4,5},{5,4},{6,7},{7,6},{8,9},{9,8},{10,11... | collective-permute-start | bytes 1572872 | tf_op jit(solution)/shard_map/ppermute | solution.py:197
  3.6 18.5 %copy-start.1 = (bf16[128,2048]{1,0:T(8,128)(2,1)S(1)}, bf16[128,2048]{1,0:T(8,128)(2,1)}, u32[]{:S(2)}) copy-start(bf16[128,2048]{1,0:T(8,128)(2,1)} %v_ref.1) | copy-start | bytes 1572868
  3.6 18.5 %copy-start.2 = (bf16[128,2048]{1,0:T(8,128)(2,1)S(1)}, bf16[128,2048]{1,0:T(8,128)(2,1)}, u32[]{:S(2)}) copy-start(bf16[128,2048]{1,0:T(8,128)(2,1)} %q_ref.4) | copy-start | bytes 1572868
  19.3 2.7 %copy-start = (bf16[128,2048]{1,0:T(8,128)(2,1)S(1)}, bf16[128,2048]{1,0:T(8,128)(2,1)}, u32[]{:S(2)}) copy-start(bf16[128,2048]{1,0:T(8,128)(2,1)} %k_ref.1) | copy-start | bytes 1572868
  19.4 5.9 %collective-permute-start.1 = (f32[128,128]{1,0:T(8,128)S(1)}, f32[128,128]{1,0:T(8,128)S(1)}, u32[]{:S(2)}, u32[]{:S(2)}) collective-permute-start(f32[128,128]{1,0:T(8,128)S(1)} %shard_map.39), channel_id=1, source_target_pairs={{0,16},{2,18},{4,20},{6,22},{8,24},{10,26},{12,28},{14,30},{16,0},... | collective-permute-start | bytes 196616 | tf_op jit(solution)/shard_map/ppermute | solution.py:220
  36.1 2.0 %collective-permute-start.2 = (f32[8,128,128]{2,1,0:T(8,128)S(1)}, f32[8,128,128]{2,1,0:T(8,128)S(1)}, u32[]{:S(2)}, u32[]{:S(2)}) collective-permute-start(f32[8,128,128]{2,1,0:T(8,128)S(1)} %shard_map.42), channel_id=1, source_target_pairs={{0,1},{1,0},{2,3},{3,2},{4,5},{5,4},{6,7},{7,6},{8,9},{9,8},{10,11... | collective-permute-start | bytes 1572872 | tf_op jit(solution)/shard_map/ppermute | solution.py:197

commit v3 on v1

v3 whole, which is shorter than its diff:
```python
import jax
import jax.numpy as jnp
from jax import lax
from jax.experimental import pallas as pl
from jax.experimental.pallas import tpu as pltpu
from jax.sharding import PartitionSpec as P

HEADS = 16
HEAD_DIM = 128
VMEM = pl.BlockSpec(memory_space=pltpu.VMEM)
HBM = pl.BlockSpec(memory_space=pltpu.HBM)
NEAR = 1
TURNS = (6, 4, 2)
LIMIT = 8 * 1024 * 1024


def call(kernel, outs, args, flops=0, ins=None, out_specs=None, scratch=()):
    moved = sum(a.size * a.dtype.itemsize for a in args)
    return pl.pallas_call(
        kernel,
        out_shape=outs,
        in_specs=ins or [VMEM] * len(args),
        out_specs=out_specs or ([VMEM] * len(outs) if isinstance(outs, list) else VMEM),
        scratch_shapes=scratch,
        compiler_params=pltpu.CompilerParams(vmem_limit_bytes=LIMIT),
        cost_estimate=pl.CostEstimate(flops=flops, bytes_accessed=moved, transcendentals=0),
    )(*args)


def f32(*shape):
    return pltpu.VMEM(shape, jnp.float32)


def head(h, first=0):
    return pl.ds(pl.multiple_of(first + h * HEAD_DIM, HEAD_DIM), HEAD_DIM)


def place_in_cube(group):
    return lax.rem(lax.axis_index("wide"), group)


def partner(core, turn, group):
    return TURNS[turn] ^ (NEAR * core)


def turns_of(group):
    return (group - 2) // 2


def heads_of(core, place, group):
    heads = []
    for turn in range(turns_of(group)):
        owner = place ^ partner(core, turn, group)
        heads += [owner, group + owner]
    return heads + [core * group + (place ^ NEAR), core * group + place]


def first_states(keys, values, group):
    tokens, width = keys.shape
    part = width // 2

    def kernel(k_hbm, v_hbm, s_ref, k_ref, v_ref, sems):
        copies = []
        for n in range(2):
            cols = slice(n * part, (n + 1) * part)
            for i, (src, dst) in enumerate(((k_hbm, k_ref), (v_hbm, v_ref))):
                copies.append(pltpu.make_async_copy(src.at[:, cols], dst.at[:, cols], sems.at[n, i]))
                copies[-1].start()
        for copy in copies:
            copy.wait()
        for n, h in enumerate(heads_of(1 - lax.axis_index("narrow"), place_in_cube(group), group)):
            s_ref[n] = state(k_ref[:, head(h)], v_ref[:, head(h)])

    return call(
        kernel,
        [f32(group, HEAD_DIM, HEAD_DIM)] + [pltpu.VMEM(keys.shape, keys.dtype)] * 2,
        (pltpu.with_memory_space_constraint(keys, pltpu.HBM), pltpu.with_memory_space_constraint(values, pltpu.HBM)),
        2 * group * tokens * HEAD_DIM * HEAD_DIM,
        ins=[HBM, HBM],
        scratch=[pltpu.SemaphoreType.DMA((2, 2))],
    )


def kept_states(keys, values, group):
    tokens = keys.shape[0]

    def kernel(k_ref, v_ref, s_ref):
        for n, h in enumerate(heads_of(lax.axis_index("narrow"), place_in_cube(group), group)):
            s_ref[n] = state(k_ref[:, head(h)], v_ref[:, head(h)])

    return call(
        kernel, f32(group, HEAD_DIM, HEAD_DIM), (keys, values), 2 * group * tokens * HEAD_DIM * HEAD_DIM
    )


def state(k, v):
    return lax.dot_general(k, v, (((0,), (0,)), ((), ())), preferred_element_type=jnp.float32)


def local_part(queries, keys, values):
    tokens = queries.shape[0]

    def kernel(q_ref, k_ref, v_ref, o_ref):
        rows = lax.broadcasted_iota(jnp.int32, (tokens, tokens), 0)
        cols = lax.broadcasted_iota(jnp.int32, (tokens, tokens), 1)
        causal = rows >= cols
        for h in range(HEADS):
            c = slice(h * HEAD_DIM, (h + 1) * HEAD_DIM)
            scores = lax.dot_general(
                q_ref[:, c], k_ref[:, c], (((1,), (1,)), ((), ())), preferred_element_type=jnp.float32
            )
            scores = jnp.where(causal, scores, 0.0).astype(jnp.bfloat16)
            o_ref[:, c] = jnp.dot(scores, v_ref[:, c], preferred_element_type=jnp.float32)

    return call(
        kernel, f32(tokens, HEADS * HEAD_DIM), (queries, keys, values), 4 * HEADS * tokens * tokens * HEAD_DIM
    )


def attended(q, local, carry):
    high = carry.astype(jnp.bfloat16)
    low = (carry - high.astype(jnp.float32)).astype(jnp.bfloat16)
    total = local + jnp.dot(
        jnp.concatenate([q, q], axis=1), jnp.concatenate([high, low], axis=0), preferred_element_type=jnp.float32
    )
    factor = lax.rsqrt(jnp.mean(total * total, axis=-1, keepdims=True) + 1e-05)
    return (total * factor).astype(jnp.bfloat16)


def finish_own(queries, local, pieces, got, group):
    tokens = queries.shape[0]
    turns = turns_of(group)

    def kernel(q_ref, l_ref, g_ref, *refs):
        o_ref = refs[-1]
        core = lax.axis_index("narrow")
        for n, h in enumerate(heads_of(core, place_in_cube(group), group)):
            carry = piece(refs, n, turns) + jnp.where(core == 1, g_ref[n], 0.0)
            o_ref[:, n * HEAD_DIM : (n + 1) * HEAD_DIM] = attended(q_ref[:, head(h)], l_ref[:, head(h)], carry)

    return call(
        kernel,
        pltpu.VMEM((tokens, group * HEAD_DIM), jnp.bfloat16),
        (queries, local, got, *pieces),
        4 * group * tokens * HEAD_DIM * HEAD_DIM,
    )


def finish_other(queries, local, carry, done, group, parts=2):
    tokens = queries.shape[0]
    rows = tokens // parts

    def kernel(q_ref, l_ref, c_ref, d_ref, o_hbm, y_ref, sems):
        core, place = lax.axis_index("narrow"), place_in_cube(group)
        for n, h in enumerate(heads_of(core, place, group)):
            y_ref[:, head(h)] = d_ref[:, n * HEAD_DIM : (n + 1) * HEAD_DIM]
        copies = []
        for p in range(parts):
            some = slice(p * rows, (p + 1) * rows)
            for n, h in enumerate(heads_of(1 - core, place, group)):
                y_ref[some, head(h)] = attended(q_ref[some, head(h)], l_ref[some, head(h)], c_ref[n])
            copies.append(pltpu.make_async_copy(y_ref.at[some, :], o_hbm.at[some, :], sems.at[p]))
            copies[-1].start()
        for copy in copies:
            copy.wait()

    return call(
        kernel,
        jax.ShapeDtypeStruct(queries.shape, jnp.bfloat16),
        (queries, local, carry, done),
        4 * group * tokens * HEAD_DIM * HEAD_DIM,
        out_specs=HBM,
        scratch=[pltpu.VMEM(queries.shape, jnp.bfloat16), pltpu.SemaphoreType.DMA((parts,))],
    )


def piece(refs, n, turns):
    return refs[n // 2][n % 2] if n < 2 * turns else refs[n - turns][...]


def chip_pieces(kept, got):
    group = kept.shape[0]
    turns = turns_of(group)

    def kernel(a_ref, b_ref, *o_refs):
        for turn in range(turns):
            for n in range(2):
                o_refs[turn][n] = a_ref[2 * turn + n] + b_ref[2 * turn + n]
        o_refs[turns][...] = a_ref[group - 2] + b_ref[group - 2]
        o_refs[turns + 1][...] = a_ref[group - 1] + b_ref[group - 1]

    shape = kept.shape[1:]
    return call(kernel, [f32(2, *shape)] * turns + [f32(*shape)] * 2, (kept, got))


def for_other_core(pairs):
    def kernel(*refs):
        other = 1 - lax.axis_index("narrow")
        for n, ref in enumerate(refs[:-1]):
            refs[-1][n] = ref[other]

    return call(kernel, f32(len(pairs), *pairs[0].shape[1:]), pairs)


def ends(core, own, far):
    return jnp.where(core == 0, own, far), jnp.where(core == 0, far, own)


def gathered(pairs, swapped, near, own):
    turns = len(pairs)

    def kernel(*refs):
        pair_refs, (s_ref, far_ref, own_ref, t_ref, p_ref) = refs[:turns], refs[turns:]
        core = lax.axis_index("narrow")
        own, far = own_ref[...], far_ref[...]
        p_ref[turns], p_ref[turns + 1] = ends(core, own, far)
        run = own + far
        for turn in range(turns):
            mine = pair_refs[turn][core]
            p_ref[turn] = mine
            run = run + mine + s_ref[turn]
        t_ref[...] = run

    shape = own.shape
    return call(kernel, [f32(*shape), f32(turns + 2, *shape)], (*pairs, swapped, near, own))


def prefix_at(blocks, corner, k):
    total, sums, bit = 0.0, blocks, 0
    while len(sums) > 1:
        inside = ((corner ^ k) >> bit & 1).astype(jnp.float32)
        total = total + sums[(k >> bit) ^ 1] * inside
        sums = [sums[i] + sums[i + 1] for i in range(0, len(sums), 2)]
        bit += 1
    return total


def cube_prefixes(pairs, swapped, near, own, received, group):
    turns = turns_of(group)
    rows = own.shape[0] // 4

    def kernel(*refs):
        pair_refs, (s_ref, far_ref, own_ref, r_ref) = refs[:turns], refs[turns : turns + 4]
        outs = refs[turns + 4 :]
        core, place = lax.axis_index("narrow"), place_in_cube(group)
        corner = place ^ (NEAR * core)
        for part in range(4):
            some = slice(part * rows, (part + 1) * rows)
            mine, other = [None] * group, [None] * group
            mine[0], mine[NEAR] = ends(core, own_ref[some], far_ref[some])
            other[NEAR], other[0] = r_ref[turns, some], r_ref[turns + 1, some]
            for turn in range(turns):
                mine[TURNS[turn]] = pair_refs[turn][core, some]
                mine[NEAR ^ TURNS[turn]] = s_ref[turn, some]
                other[TURNS[turn]] = pair_refs[turn][1 - core, some]
                other[NEAR ^ TURNS[turn]] = r_ref[turn, some]
            for turn in range(turns):
                outs[turn][core, some] = prefix_at(mine, corner, TURNS[turn])
                outs[turn][1 - core, some] = prefix_at(other, corner, TURNS[turn])
            own_sum, far_sum = ends(core, prefix_at(mine, corner, 0), prefix_at(mine, corner, NEAR))
            outs[turns][some] = far_sum
            outs[turns + 1][some] = own_sum

    shape = own.shape
    return call(
        kernel, [f32(2, *shape)] * turns + [f32(*shape)] * 2, (*pairs, swapped, near, own, received)
    )


def add_earlier(pieces, earlier, others, upper_only, group):
    count = len(pieces)

    def kernel(e_ref, o_ref, *refs):
        core = lax.axis_index("narrow")
        mine, other = e_ref[...], o_ref[...]
        if upper_only:
            upper = lax.axis_index("wide") >= group
            mine, other = jnp.where(upper, mine, 0.0), jnp.where(upper, other, 0.0)
        for ref, out in zip(refs[:count], refs[count:]):
            if len(ref.shape) == 3:
                out[core] = ref[core] + mine
                out[1 - core] = ref[1 - core] + other
            else:
                out[...] = ref[...] + mine

    return call(kernel, [f32(*piece.shape) for piece in pieces], (earlier, others, *pieces))


def add_lower(pieces, kept):
    group = kept.shape[0]
    turns = turns_of(group)

    def kernel(k_ref, *refs):
        lower = lax.axis_index("narrow") == 0
        for n in range(group):
            refs[-1][n] = piece(refs, n, turns) + jnp.where(lower, k_ref[n], 0.0)

    return call(kernel, f32(*kept.shape), (kept, *pieces))


def swap_cores(block):
    return lax.ppermute(block, "narrow", [(0, 1), (1, 0)])


def pair_chips(block, chips, cores, of):
    route = [(i * cores + c, (i ^ of(c)) * cores + c) for i in range(chips) for c in range(cores)]
    return lax.ppermute(block, ("wide", "narrow"), route)


def pairings(pairs, near, chips, cores, group):
    pairs = [
        pair_chips(pair, chips, cores, lambda c, turn=turn: partner(c, turn, group)) for turn, pair in enumerate(pairs)
    ]
    return pairs, pair_chips(near, chips, cores, lambda c: NEAR)


def shards(queries, keys, values):
    chips, cores = lax.axis_size("wide"), lax.axis_size("narrow")
    group = HEADS // cores
    groups = chips // group

    given, keys, values = first_states(keys, values, group)
    got = swap_cores(given)
    kept = kept_states(keys, values, group)
    *pairs, near, mine = chip_pieces(kept, got)
    later_q, _ = lax.optimization_barrier((queries, mine))
    pairs, near = pairings(pairs, near, chips, cores, group)
    local = local_part(later_q, keys, values)
    *pairs, near, local = lax.optimization_barrier((*pairs, near, local))
    swapped = swap_cores(for_other_core(pairs))
    running, lacking = gathered(pairs, swapped, near, mine)
    cube = lax.axis_index("wide") // group
    earlier = jnp.zeros_like(running) if groups != 2 else None
    step = 1
    while step < groups:
        seen = lax.ppermute(running, "wide", [(i, i ^ (step * group)) for i in range(chips)])
        earlier = seen if groups == 2 else earlier + jnp.where((cube & step) != 0, seen, 0.0)
        running = running + seen
        step *= 2
    received = swap_cores(lacking)
    earlier, received = lax.optimization_barrier((earlier, received))
    others = swap_cores(earlier)
    pieces = cube_prefixes(pairs, swapped, near, mine, received, group)
    others, *pieces = lax.optimization_barrier((others, *pieces))
    *pairs, far, mine = add_earlier(pieces, earlier, others, groups == 2, group)
    pairs, far = pairings(pairs, far, chips, cores, group)
    pieces = lax.optimization_barrier((*pairs, far, mine))
    other = swap_cores(add_lower(pieces, kept))
    own = finish_own(queries, local, pieces, got, group)
    return finish_other(queries, local, other, own, group)


def solution(mesh):
    placed = P(("wide", "narrow"), None)
    return jax.shard_map(
        shards, mesh=mesh, in_specs=(placed, placed, placed), out_specs=placed, check_vma=False
    )
```

time: 43.7 us -> 38.4 us (0.88)
  blocking collectives: 15.6 us -> 0 us
  starting transfers between devices: 6.87 us -> 16.6 us
  waiting for transfers between devices: 12.1 us -> 15.3 us
  local copies, waits for them, and re-layouts: 2.1 us -> 0.01 us
  other arithmetic: 0.9 us -> 0 us
  Pallas kernels: 5.68 us -> 6.31 us
    all_to_all x1 -> x0, blocking collectives: 15.6 us -> none  [shards(): lax.all_to_all(chip, 'wide', 0, 0, axis_index_groups=cubes, tiled=True)]
    ppermute x1 -> x9, starting transfers between devices: 2.65 us -> 14.7 us  [the longest x8 12.1 us: pair_chips(): return lax.ppermute(block, ('wide', 'narrow'), route)]
    all_to_all x1 -> x0, waiting for transfers between devices: 7.53 us -> none  [shards(): lax.all_to_all(before + earlier, 'wide', 0, 0, axis_index_groups=cubes, t...]
    ppermute x1 -> x9, waiting for transfers between devices: 3.28 us -> 10.8 us  [the longest x8 6.83 us: pair_chips(): return lax.ppermute(block, ('wide', 'narrow'), route)]
    all_to_all x1 -> x0, starting transfers between devices: 3.63 us -> none  [shards(): lax.all_to_all(before + earlier, 'wide', 0, 0, axis_index_groups=cubes, t...]
    ppermute x3 -> x5, waiting for transfers between devices: 1.25 us -> 4.56 us  [swap_cores(): return lax.ppermute(block, 'narrow', [(0, 1), (1, 0)])]
    unnamed x10 -> x2, local copies, waits for them, and re-layouts: 2.1 us -> 0.01 us
    ppermute x3 -> x5, starting transfers between devices: 0.59 us -> 1.89 us  [swap_cores(): return lax.ppermute(block, 'narrow', [(0, 1), (1, 0)])]
  transfers between devices with their start and end apart: 5 -> 14, of which waited for: 3 -> 9; matrix products, arithmetic and copies ran while one was open for 0% -> 0% of each run, Pallas kernels for 7% -> 9%
where the time goes in v3:
time: 38.4 us; the launch traced here: 38.3 us
  starting transfers between devices  16.6 us (43%)
  waiting for transfers between devices  15.3 us (40%)
  Pallas kernels  6.31 us (16%)
    ppermute x8, starting transfers between devices, pair_chips(): return lax.ppermute(block, ('wide', 'narrow'), route)  12.1 us
    ppermute x8, waiting for transfers between devices, pair_chips(): return lax.ppermute(block, ('wide', 'narrow'), route)  6.83 us
    pallas_call x11, Pallas kernels, call(): pl.pallas_call(kernel, out_shape=outs, in_specs=ins or [VMEM] * len(args)...  6.31 us
    ppermute x5, waiting for transfers between devices, swap_cores(): return lax.ppermute(block, 'narrow', [(0, 1), (1, 0)])  4.56 us
    ppermute x1, waiting for transfers between devices, shards(): lax.ppermute(running, 'wide', [(i, i ^ step * group) for i in range(chips)])  3.93 us
    ppermute x1, starting transfers between devices, shards(): lax.ppermute(running, 'wide', [(i, i ^ step * group) for i in range(chips)])  2.64 us
    ppermute x5, starting transfers between devices, swap_cores(): return lax.ppermute(block, 'narrow', [(0, 1), (1, 0)])  1.89 us
  transfers between devices with their start and end apart: 14, of which 9 were waited for; matrix products, arithmetic and copies ran while one was open for 0% of the time, Pallas kernels for 9%

profile of v3, /device:TPU:0, one launch (start us, length us, event | category | flops | bytes accessed | tf_op | source)
XLA Modules:
  0.0 38.3 jit_solution(9684109809774077926)
XLA Ops:
  0.0 1.5 %shard_map.37 = (f32[8,128,128]{2,1,0:T(8,128)S(1)}, bf16[128,2048]{1,0:T(8,128)(2,1)S(1)}, bf16[128,2048]{1,0:T(8,128)(2,1)S(1)}) custom-call(bf16[128,2048]{1,0:T(8,128)(2,1)} %k_hbm.1, bf16[128,2048]{1,0:T(8,128)(2,1)} %v_hbm.1), custom_call_target="tpu_custom_call" | custom-call | flops 33554432 | bytes 1048576 | tf_op jit(solution)/shard_map/pallas_call | solution.py:19
  1.5 0.5 %collective-permute-start = (f32[8,128,128]{2,1,0:T(8,128)S(1)}, f32[8,128,128]{2,1,0:T(8,128)S(1)}, u32[]{:S(2)}, u32[]{:S(2)}) collective-permute-start(f32[8,128,128]{2,1,0:T(8,128)S(1)} %get-tuple-element.46), channel_id=1, source_target_pairs={{0,1},{1,0},{2,3},{3,2},{4,5},{5,4},{6,7},{7,6},{8,9},{9,8},{10,11... | collective-permute-start | bytes 1572872 | tf_op jit(solution)/shard_map/ppermute | solution.py:302
  2.3 1.2 %collective-permute-done.b_ref.g_ref = f32[8,128,128]{2,1,0:T(8,128)S(1)} collective-permute-done((f32[8,128,128]{2,1,0:T(8,128)S(1)}, f32[8,128,128]{2,1,0:T(8,128)S(1)}, u32[]{:S(2)}, u32[]{:S(2)}) %collective-permute-start) | collective-permute-done | bytes 524320 | tf_op jit(solution)/shard_map/ppermute | solution.py:302
  3.6 4.0 %collective-permute-start.1 = (f32[2,128,128]{2,1,0:T(8,128)S(1)}, f32[2,128,128]{2,1,0:T(8,128)S(1)}, u32[]{:S(2)}, u32[]{:S(2)}) collective-permute-start(f32[2,128,128]{2,1,0:T(8,128)S(1)} %get-tuple-element.47), channel_id=1, source_target_pairs={{0,12},{1,15},{2,14},{3,13},{4,8},{5,11},{6,10},{7,9},{8,4},{9,7},... | collective-permute-start | bytes 393224 | tf_op jit(solution)/shard_map/ppermute | solution.py:307
  7.6 0.4 %collective-permute-start.2 = (f32[2,128,128]{2,1,0:T(8,128)S(1)}, f32[2,128,128]{2,1,0:T(8,128)S(1)}, u32[]{:S(2)}, u32[]{:S(2)}) collective-permute-start(f32[2,128,128]{2,1,0:T(8,128)S(1)} %get-tuple-element.48), channel_id=1, source_target_pairs={{0,8},{1,11},{2,10},{3,9},{4,12},{5,15},{6,14},{7,13},{8,0},{9,3},... | collective-permute-start | bytes 393224 | tf_op jit(solution)/shard_map/ppermute | solution.py:307
  8.2 1.8 %collective-permute-start.4 = (f32[128,128]{1,0:T(8,128)S(1)}, f32[128,128]{1,0:T(8,128)S(1)}, u32[]{:S(2)}, u32[]{:S(2)}) collective-permute-start(f32[128,128]{1,0:T(8,128)S(1)} %get-tuple-element.50), channel_id=1, source_target_pairs={{0,2},{1,3},{2,0},{3,1},{4,6},{5,7},{6,4},{7,5},{8,10},{9,11},{10,... | collective-permute-start | bytes 196616 | tf_op jit(solution)/shard_map/ppermute | solution.py:307
  10.1 2.6 %shard_map.40.l_ref = f32[128,2048]{1,0:T(8,128)S(1)} custom-call(bf16[128,2048]{1,0:T(8,128)(2,1)S(1)} %copy-done, bf16[128,2048]{1,0:T(8,128)(2,1)S(1)} %get-tuple-element.44.k_ref, bf16[128,2048]{1,0:T(8,128)(2,1)S(1)} %get-tuple-element.45.v_ref), custom_call_target="tpu_custom_call" | custom-call | flops 134217728 | bytes 1572864 | tf_op jit(solution)/shard_map/pallas_call | solution.py:19
  12.6 1.9 %collective-permute-done.4.refs_4_ = f32[128,128]{1,0:T(8,128)S(1)} collective-permute-done((f32[128,128]{1,0:T(8,128)S(1)}, f32[128,128]{1,0:T(8,128)S(1)}, u32[]{:S(2)}, u32[]{:S(2)}) %collective-permute-start.4) | collective-permute-done | bytes 65568 | tf_op jit(solution)/shard_map/ppermute | solution.py:307
  14.5 0.6 %collective-permute-done.2.refs_1_ = f32[2,128,128]{2,1,0:T(8,128)S(1)} collective-permute-done((f32[2,128,128]{2,1,0:T(8,128)S(1)}, f32[2,128,128]{2,1,0:T(8,128)S(1)}, u32[]{:S(2)}, u32[]{:S(2)}) %collective-permute-start.2) | collective-permute-done | bytes 131104 | tf_op jit(solution)/shard_map/ppermute | solution.py:307
  15.1 0.5 %collective-permute-start.5 = (f32[3,128,128]{2,1,0:T(8,128)S(1)}, f32[3,128,128]{2,1,0:T(8,128)S(1)}, u32[]{:S(2)}, u32[]{:S(2)}) collective-permute-start(f32[3,128,128]{2,1,0:T(8,128)S(1)} %shard_map.41), channel_id=1, source_target_pairs={{0,1},{1,0},{2,3},{3,2},{4,5},{5,4},{6,7},{7,6},{8,9},{9,8},{10,11... | collective-permute-start | bytes 589832 | tf_op jit(solution)/shard_map/ppermute | solution.py:302
  15.6 1.1 %collective-permute-done.5.refs_3_ = f32[3,128,128]{2,1,0:T(8,128)S(1)} collective-permute-done((f32[3,128,128]{2,1,0:T(8,128)S(1)}, f32[3,128,128]{2,1,0:T(8,128)S(1)}, u32[]{:S(2)}, u32[]{:S(2)}) %collective-permute-start.5) | collective-permute-done | bytes 196640 | tf_op jit(solution)/shard_map/ppermute | solution.py:302
  16.7 0.4 %collective-permute-start.7 = (f32[5,128,128]{2,1,0:T(8,128)S(1)}, f32[5,128,128]{2,1,0:T(8,128)S(1)}, u32[]{:S(2)}, u32[]{:S(2)}) collective-permute-start(f32[5,128,128]{2,1,0:T(8,128)S(1)} %get-tuple-element.59), channel_id=1, source_target_pairs={{0,1},{1,0},{2,3},{3,2},{4,5},{5,4},{6,7},{7,6},{8,9},{9,8},{10,11... | collective-permute-start | bytes 983048 | tf_op jit(solution)/shard_map/ppermute | solution.py:302
  17.2 2.6 %collective-permute-start.6 = (f32[128,128]{1,0:T(8,128)S(1)}, f32[128,128]{1,0:T(8,128)S(1)}, u32[]{:S(2)}, u32[]{:S(2)}) collective-permute-start(f32[128,128]{1,0:T(8,128)S(1)} %get-tuple-element.58), channel_id=1, source_target_pairs={{0,16},{2,18},{4,20},{6,22},{8,24},{10,26},{12,28},{14,30},{16,0},... | collective-permute-start | bytes 196616 | tf_op jit(solution)/shard_map/ppermute | solution.py:336
  19.8 3.9 %collective-permute-done.6.e_ref = f32[128,128]{1,0:T(8,128)S(1)} collective-permute-done((f32[128,128]{1,0:T(8,128)S(1)}, f32[128,128]{1,0:T(8,128)S(1)}, u32[]{:S(2)}, u32[]{:S(2)}) %collective-permute-start.6) | collective-permute-done | bytes 65568 | tf_op jit(solution)/shard_map/ppermute | solution.py:336
  23.9 1.1 %collective-permute-done.8.o_ref = f32[128,128]{1,0:T(8,128)S(1)} collective-permute-done((f32[128,128]{1,0:T(8,128)S(1)}, f32[128,128]{1,0:T(8,128)S(1)}, u32[]{:S(2)}, u32[]{:S(2)}) %collective-permute-start.8) | collective-permute-done | bytes 65568 | tf_op jit(solution)/shard_map/ppermute | solution.py:302
  25.0 1.6 %collective-permute-start.9 = (f32[2,128,128]{2,1,0:T(8,128)S(1)}, f32[2,128,128]{2,1,0:T(8,128)S(1)}, u32[]{:S(2)}, u32[]{:S(2)}) collective-permute-start(f32[2,128,128]{2,1,0:T(8,128)S(1)} %get-tuple-element.73), channel_id=1, source_target_pairs={{0,12},{1,15},{2,14},{3,13},{4,8},{5,11},{6,10},{7,9},{8,4},{9,7},... | collective-permute-start | bytes 393224 | tf_op jit(solution)/shard_map/ppermute | solution.py:307
  26.6 1.3 %collective-permute-start.10 = (f32[2,128,128]{2,1,0:T(8,128)S(1)}, f32[2,128,128]{2,1,0:T(8,128)S(1)}, u32[]{:S(2)}, u32[]{:S(2)}) collective-permute-start(f32[2,128,128]{2,1,0:T(8,128)S(1)} %get-tuple-element.74), channel_id=1, source_target_pairs={{0,8},{1,11},{2,10},{3,9},{4,12},{5,15},{6,14},{7,13},{8,0},{9,3},... | collective-permute-start | bytes 393224 | tf_op jit(solution)/shard_map/ppermute | solution.py:307
  27.9 0.6 %collective-permute-start.11 = (f32[2,128,128]{2,1,0:T(8,128)S(1)}, f32[2,128,128]{2,1,0:T(8,128)S(1)}, u32[]{:S(2)}, u32[]{:S(2)}) collective-permute-start(f32[2,128,128]{2,1,0:T(8,128)S(1)} %get-tuple-element.75), channel_id=1, source_target_pairs={{0,4},{1,7},{2,6},{3,5},{4,0},{5,3},{6,2},{7,1},{8,12},{9,15},{10,... | collective-permute-start | bytes 393224 | tf_op jit(solution)/shard_map/ppermute | solution.py:307
  28.6 2.1 %collective-permute-start.12 = (f32[128,128]{1,0:T(8,128)S(1)}, f32[128,128]{1,0:T(8,128)S(1)}, u32[]{:S(2)}, u32[]{:S(2)}) collective-permute-start(f32[128,128]{1,0:T(8,128)S(1)} %get-tuple-element.76), channel_id=1, source_target_pairs={{0,2},{1,3},{2,0},{3,1},{4,6},{5,7},{6,4},{7,5},{8,10},{9,11},{10,... | collective-permute-start | bytes 196616 | tf_op jit(solution)/shard_map/ppermute | solution.py:307
  30.7 4.1 %collective-permute-done.12.refs_3_ = f32[128,128]{1,0:T(8,128)S(1)} collective-permute-done((f32[128,128]{1,0:T(8,128)S(1)}, f32[128,128]{1,0:T(8,128)S(1)}, u32[]{:S(2)}, u32[]{:S(2)}) %collective-permute-start.12) | collective-permute-done | bytes 65568 | tf_op jit(solution)/shard_map/ppermute | solution.py:307
  35.1 0.4 %collective-permute-start.13 = (f32[8,128,128]{2,1,0:T(8,128)S(1)}, f32[8,128,128]{2,1,0:T(8,128)S(1)}, u32[]{:S(2)}, u32[]{:S(2)}) collective-permute-start(f32[8,128,128]{2,1,0:T(8,128)S(1)} %shard_map.45), channel_id=1, source_target_pairs={{0,1},{1,0},{2,3},{3,2},{4,5},{5,4},{6,7},{7,6},{8,9},{9,8},{10,11... | collective-permute-start | bytes 1572872 | tf_op jit(solution)/shard_map/ppermute | solution.py:302
  35.6 0.4 %shard_map.46.d_ref = bf16[128,1024]{1,0:T(8,128)(2,1)S(1)} custom-call(bf16[128,2048]{1,0:T(8,128)(2,1)S(1)} %copy-done, f32[128,2048]{1,0:T(8,128)S(1)} %shard_map.40.l_ref, f32[8,128,128]{2,1,0:T(8,128)S(1)} %collective-permute-done.b_ref.g_ref, f32[2,128,128]{2,1,0:T(8,128)S(1)} %collective-permute-done.9.refs_0_, ...), custom_call_target="tpu_custom_call" | custom-call | flops 67108864 | bytes 2621440 | tf_op jit(solution)/shard_map/pallas_call | solution.py:19
  36.0 1.1 %collective-permute-done.13.c_ref = f32[8,128,128]{2,1,0:T(8,128)S(1)} collective-permute-done((f32[8,128,128]{2,1,0:T(8,128)S(1)}, f32[8,128,128]{2,1,0:T(8,128)S(1)}, u32[]{:S(2)}, u32[]{:S(2)}) %collective-permute-start.13) | collective-permute-done | bytes 524320 | tf_op jit(solution)/shard_map/ppermute | solution.py:302
  37.1 1.2 %shard_map.47 = bf16[128,2048]{1,0:T(8,128)(2,1)} custom-call(bf16[128,2048]{1,0:T(8,128)(2,1)S(1)} %copy-done, f32[128,2048]{1,0:T(8,128)S(1)} %shard_map.40.l_ref, f32[8,128,128]{2,1,0:T(8,128)S(1)} %collective-permute-done.13.c_ref, bf16[128,1024]{1,0:T(8,128)(2,1)S(1)} %shard_map.46.d_ref), custom_call_target="tpu_custom_call" | custom-call | flops 67108864 | bytes 2359296 | tf_op jit(solution)/shard_map/pallas_call | solution.py:19
  (17 shorter events, 1.1 us)
Async XLA Ops:
  1.5 2.1 %collective-permute-start = (f32[8,128,128]{2,1,0:T(8,128)S(1)}, f32[8,128,128]{2,1,0:T(8,128)S(1)}, u32[]{:S(2)}, u32[]{:S(2)}) collective-permute-start(f32[8,128,128]{2,1,0:T(8,128)S(1)} %get-tuple-element.46), channel_id=1, source_target_pairs={{0,1},{1,0},{2,3},{3,2},{4,5},{5,4},{6,7},{7,6},{8,9},{9,8},{10,11... | collective-permute-start | bytes 1572872 | tf_op jit(solution)/shard_map/ppermute | solution.py:302
  2.3 7.7 %copy-start = (bf16[128,2048]{1,0:T(8,128)(2,1)S(1)}, bf16[128,2048]{1,0:T(8,128)(2,1)}, u32[]{:S(2)}) copy-start(bf16[128,2048]{1,0:T(8,128)(2,1)} %q_ref.4) | copy-start | bytes 1572868
  3.6 10.8 %collective-permute-start.1 = (f32[2,128,128]{2,1,0:T(8,128)S(1)}, f32[2,128,128]{2,1,0:T(8,128)S(1)}, u32[]{:S(2)}, u32[]{:S(2)}) collective-permute-start(f32[2,128,128]{2,1,0:T(8,128)S(1)} %get-tuple-element.47), channel_id=1, source_target_pairs={{0,12},{1,15},{2,14},{3,13},{4,8},{5,11},{6,10},{7,9},{8,4},{9,7},... | collective-permute-start | bytes 393224 | tf_op jit(solution)/shard_map/ppermute | solution.py:307
  7.6 7.5 %collective-permute-start.2 = (f32[2,128,128]{2,1,0:T(8,128)S(1)}, f32[2,128,128]{2,1,0:T(8,128)S(1)}, u32[]{:S(2)}, u32[]{:S(2)}) collective-permute-start(f32[2,128,128]{2,1,0:T(8,128)S(1)} %get-tuple-element.48), channel_id=1, source_target_pairs={{0,8},{1,11},{2,10},{3,9},{4,12},{5,15},{6,14},{7,13},{8,0},{9,3},... | collective-permute-start | bytes 393224 | tf_op jit(solution)/shard_map/ppermute | solution.py:307
  8.0 7.1 %collective-permute-start.3 = (f32[2,128,128]{2,1,0:T(8,128)S(1)}, f32[2,128,128]{2,1,0:T(8,128)S(1)}, u32[]{:S(2)}, u32[]{:S(2)}) collective-permute-start(f32[2,128,128]{2,1,0:T(8,128)S(1)} %get-tuple-element.49), channel_id=1, source_target_pairs={{0,4},{1,7},{2,6},{3,5},{4,0},{5,3},{6,2},{7,1},{8,12},{9,15},{10,... | collective-permute-start | bytes 393224 | tf_op jit(solution)/shard_map/ppermute | solution.py:307
  8.2 6.2 %collective-permute-start.4 = (f32[128,128]{1,0:T(8,128)S(1)}, f32[128,128]{1,0:T(8,128)S(1)}, u32[]{:S(2)}, u32[]{:S(2)}) collective-permute-start(f32[128,128]{1,0:T(8,128)S(1)} %get-tuple-element.50), channel_id=1, source_target_pairs={{0,2},{1,3},{2,0},{3,1},{4,6},{5,7},{6,4},{7,5},{8,10},{9,11},{10,... | collective-permute-start | bytes 196616 | tf_op jit(solution)/shard_map/ppermute | solution.py:307
  15.1 1.6 %collective-permute-start.5 = (f32[3,128,128]{2,1,0:T(8,128)S(1)}, f32[3,128,128]{2,1,0:T(8,128)S(1)}, u32[]{:S(2)}, u32[]{:S(2)}) collective-permute-start(f32[3,128,128]{2,1,0:T(8,128)S(1)} %shard_map.41), channel_id=1, source_target_pairs={{0,1},{1,0},{2,3},{3,2},{4,5},{5,4},{6,7},{7,6},{8,9},{9,8},{10,11... | collective-permute-start | bytes 589832 | tf_op jit(solution)/shard_map/ppermute | solution.py:302
  16.7 7.0 %collective-permute-start.7 = (f32[5,128,128]{2,1,0:T(8,128)S(1)}, f32[5,128,128]{2,1,0:T(8,128)S(1)}, u32[]{:S(2)}, u32[]{:S(2)}) collective-permute-start(f32[5,128,128]{2,1,0:T(8,128)S(1)} %get-tuple-element.59), channel_id=1, source_target_pairs={{0,1},{1,0},{2,3},{3,2},{4,5},{5,4},{6,7},{7,6},{8,9},{9,8},{10,11... | collective-permute-start | bytes 983048 | tf_op jit(solution)/shard_map/ppermute | solution.py:302
  17.2 6.6 %collective-permute-start.6 = (f32[128,128]{1,0:T(8,128)S(1)}, f32[128,128]{1,0:T(8,128)S(1)}, u32[]{:S(2)}, u32[]{:S(2)}) collective-permute-start(f32[128,128]{1,0:T(8,128)S(1)} %get-tuple-element.58), channel_id=1, source_target_pairs={{0,16},{2,18},{4,20},{6,22},{8,24},{10,26},{12,28},{14,30},{16,0},... | collective-permute-start | bytes 196616 | tf_op jit(solution)/shard_map/ppermute | solution.py:336
  23.7 1.3 %collective-permute-start.8 = (f32[128,128]{1,0:T(8,128)S(1)}, f32[128,128]{1,0:T(8,128)S(1)}, u32[]{:S(2)}, u32[]{:S(2)}) collective-permute-start(f32[128,128]{1,0:T(8,128)S(1)} %collective-permute-done.6.e_ref), channel_id=1, source_target_pairs={{0,1},{1,0},{2,3},{3,2},{4,5},{5,4},{6,7},{7,6},{8,9},{9,8},{10,11... | collective-permute-start | bytes 196616 | tf_op jit(solution)/shard_map/ppermute | solution.py:302
  25.0 9.7 %collective-permute-start.9 = (f32[2,128,128]{2,1,0:T(8,128)S(1)}, f32[2,128,128]{2,1,0:T(8,128)S(1)}, u32[]{:S(2)}, u32[]{:S(2)}) collective-permute-start(f32[2,128,128]{2,1,0:T(8,128)S(1)} %get-tuple-element.73), channel_id=1, source_target_pairs={{0,12},{1,15},{2,14},{3,13},{4,8},{5,11},{6,10},{7,9},{8,4},{9,7},... | collective-permute-start | bytes 393224 | tf_op jit(solution)/shard_map/ppermute | solution.py:307
  26.6 8.4 %collective-permute-start.10 = (f32[2,128,128]{2,1,0:T(8,128)S(1)}, f32[2,128,128]{2,1,0:T(8,128)S(1)}, u32[]{:S(2)}, u32[]{:S(2)}) collective-permute-start(f32[2,128,128]{2,1,0:T(8,128)S(1)} %get-tuple-element.74), channel_id=1, source_target_pairs={{0,8},{1,11},{2,10},{3,9},{4,12},{5,15},{6,14},{7,13},{8,0},{9,3},... | collective-permute-start | bytes 393224 | tf_op jit(solution)/shard_map/ppermute | solution.py:307
  27.9 7.1 %collective-permute-start.11 = (f32[2,128,128]{2,1,0:T(8,128)S(1)}, f32[2,128,128]{2,1,0:T(8,128)S(1)}, u32[]{:S(2)}, u32[]{:S(2)}) collective-permute-start(f32[2,128,128]{2,1,0:T(8,128)S(1)} %get-tuple-element.75), channel_id=1, source_target_pairs={{0,4},{1,7},{2,6},{3,5},{4,0},{5,3},{6,2},{7,1},{8,12},{9,15},{10,... | collective-permute-start | bytes 393224 | tf_op jit(solution)/shard_map/ppermute | solution.py:307
  28.6 6.1 %collective-permute-start.12 = (f32[128,128]{1,0:T(8,128)S(1)}, f32[128,128]{1,0:T(8,128)S(1)}, u32[]{:S(2)}, u32[]{:S(2)}) collective-permute-start(f32[128,128]{1,0:T(8,128)S(1)} %get-tuple-element.76), channel_id=1, source_target_pairs={{0,2},{1,3},{2,0},{3,1},{4,6},{5,7},{6,4},{7,5},{8,10},{9,11},{10,... | collective-permute-start | bytes 196616 | tf_op jit(solution)/shard_map/ppermute | solution.py:307
  35.1 2.0 %collective-permute-start.13 = (f32[8,128,128]{2,1,0:T(8,128)S(1)}, f32[8,128,128]{2,1,0:T(8,128)S(1)}, u32[]{:S(2)}, u32[]{:S(2)}) collective-permute-start(f32[8,128,128]{2,1,0:T(8,128)S(1)} %shard_map.45), channel_id=1, source_target_pairs={{0,1},{1,0},{2,3},{3,2},{4,5},{5,4},{6,7},{7,6},{8,9},{9,8},{10,11... | collective-permute-start | bytes 1572872 | tf_op jit(solution)/shard_map/ppermute | solution.py:302

commit v4 on v3

--- a/solution.py
+++ b/solution.py
@@ -10,7 +10,6 @@
 VMEM = pl.BlockSpec(memory_space=pltpu.VMEM)
 HBM = pl.BlockSpec(memory_space=pltpu.HBM)
 NEAR = 1
-TURNS = (6, 4, 2)
 LIMIT = 8 * 1024 * 1024
 
 
@@ -40,7 +39,7 @@
 
 
 def partner(core, turn, group):
-    return TURNS[turn] ^ (NEAR * core)
+    return (group - 2 * (turn + 1)) ^ (NEAR * core)
 
 
 def turns_of(group):
@@ -250,13 +249,13 @@
             mine[0], mine[NEAR] = ends(core, own_ref[some], far_ref[some])
             other[NEAR], other[0] = r_ref[turns, some], r_ref[turns + 1, some]
             for turn in range(turns):
-                mine[TURNS[turn]] = pair_refs[turn][core, some]
-                mine[NEAR ^ TURNS[turn]] = s_ref[turn, some]
-                other[TURNS[turn]] = pair_refs[turn][1 - core, some]
-                other[NEAR ^ TURNS[turn]] = r_ref[turn, some]
+                mine[partner(0, turn, group)] = pair_refs[turn][core, some]
+                mine[NEAR ^ partner(0, turn, group)] = s_ref[turn, some]
+                other[partner(0, turn, group)] = pair_refs[turn][1 - core, some]
+                other[NEAR ^ partner(0, turn, group)] = r_ref[turn, some]
             for turn in range(turns):
-                outs[turn][core, some] = prefix_at(mine, corner, TURNS[turn])
-                outs[turn][1 - core, some] = prefix_at(other, corner, TURNS[turn])
+                outs[turn][core, some] = prefix_at(mine, corner, partner(0, turn, group))
+                outs[turn][1 - core, some] = prefix_at(other, corner, partner(0, turn, group))
             own_sum, far_sum = ends(core, prefix_at(mine, corner, 0), prefix_at(mine, corner, NEAR))
             outs[turns][some] = far_sum
             outs[turns + 1][some] = own_sum

time: 38.4 us -> 38.4 us (level)
  no operation moved by 1% of the time
where the time goes in v4:
time: 38.4 us; the launch traced here: 38.3 us
  starting transfers between devices  16.6 us (43%)
  waiting for transfers between devices  15.3 us (40%)
  Pallas kernels  6.31 us (16%)
    ppermute x8, starting transfers between devices, pair_chips(): return lax.ppermute(block, ('wide', 'narrow'), route)  12.1 us
    ppermute x8, waiting for transfers between devices, pair_chips(): return lax.ppermute(block, ('wide', 'narrow'), route)  6.83 us
    pallas_call x11, Pallas kernels, call(): pl.pallas_call(kernel, out_shape=outs, in_specs=ins or [VMEM] * len(args)...  6.31 us
    ppermute x5, waiting for transfers between devices, swap_cores(): return lax.ppermute(block, 'narrow', [(0, 1), (1, 0)])  4.56 us
    ppermute x1, waiting for transfers between devices, shards(): lax.ppermute(running, 'wide', [(i, i ^ step * group) for i in range(chips)])  3.93 us
    ppermute x1, starting transfers between devices, shards(): lax.ppermute(running, 'wide', [(i, i ^ step * group) for i in range(chips)])  2.64 us
    ppermute x5, starting transfers between devices, swap_cores(): return lax.ppermute(block, 'narrow', [(0, 1), (1, 0)])  1.89 us
  transfers between devices with their start and end apart: 14, of which 9 were waited for; matrix products, arithmetic and copies ran while one was open for 0% of the time, Pallas kernels for 9%

profile of v4, /device:TPU:0, one launch (start us, length us, event | category | flops | bytes accessed | tf_op | source)
XLA Modules:
  0.0 38.3 jit_solution(9684109809774077926)
XLA Ops:
  0.0 1.5 %shard_map.37 = (f32[8,128,128]{2,1,0:T(8,128)S(1)}, bf16[128,2048]{1,0:T(8,128)(2,1)S(1)}, bf16[128,2048]{1,0:T(8,128)(2,1)S(1)}) custom-call(bf16[128,2048]{1,0:T(8,128)(2,1)} %k_hbm.1, bf16[128,2048]{1,0:T(8,128)(2,1)} %v_hbm.1), custom_call_target="tpu_custom_call" | custom-call | flops 33554432 | bytes 1048576 | tf_op jit(solution)/shard_map/pallas_call | solution.py:18
  1.5 0.5 %collective-permute-start = (f32[8,128,128]{2,1,0:T(8,128)S(1)}, f32[8,128,128]{2,1,0:T(8,128)S(1)}, u32[]{:S(2)}, u32[]{:S(2)}) collective-permute-start(f32[8,128,128]{2,1,0:T(8,128)S(1)} %get-tuple-element.46), channel_id=1, source_target_pairs={{0,1},{1,0},{2,3},{3,2},{4,5},{5,4},{6,7},{7,6},{8,9},{9,8},{10,11... | collective-permute-start | bytes 1572872 | tf_op jit(solution)/shard_map/ppermute | solution.py:301
  2.3 1.2 %collective-permute-done.b_ref.g_ref = f32[8,128,128]{2,1,0:T(8,128)S(1)} collective-permute-done((f32[8,128,128]{2,1,0:T(8,128)S(1)}, f32[8,128,128]{2,1,0:T(8,128)S(1)}, u32[]{:S(2)}, u32[]{:S(2)}) %collective-permute-start) | collective-permute-done | bytes 524320 | tf_op jit(solution)/shard_map/ppermute | solution.py:301
  3.6 4.0 %collective-permute-start.1 = (f32[2,128,128]{2,1,0:T(8,128)S(1)}, f32[2,128,128]{2,1,0:T(8,128)S(1)}, u32[]{:S(2)}, u32[]{:S(2)}) collective-permute-start(f32[2,128,128]{2,1,0:T(8,128)S(1)} %get-tuple-element.47), channel_id=1, source_target_pairs={{0,12},{1,15},{2,14},{3,13},{4,8},{5,11},{6,10},{7,9},{8,4},{9,7},... | collective-permute-start | bytes 393224 | tf_op jit(solution)/shard_map/ppermute | solution.py:306
  7.6 0.4 %collective-permute-start.2 = (f32[2,128,128]{2,1,0:T(8,128)S(1)}, f32[2,128,128]{2,1,0:T(8,128)S(1)}, u32[]{:S(2)}, u32[]{:S(2)}) collective-permute-start(f32[2,128,128]{2,1,0:T(8,128)S(1)} %get-tuple-element.48), channel_id=1, source_target_pairs={{0,8},{1,11},{2,10},{3,9},{4,12},{5,15},{6,14},{7,13},{8,0},{9,3},... | collective-permute-start | bytes 393224 | tf_op jit(solution)/shard_map/ppermute | solution.py:306
  8.2 1.8 %collective-permute-start.4 = (f32[128,128]{1,0:T(8,128)S(1)}, f32[128,128]{1,0:T(8,128)S(1)}, u32[]{:S(2)}, u32[]{:S(2)}) collective-permute-start(f32[128,128]{1,0:T(8,128)S(1)} %get-tuple-element.50), channel_id=1, source_target_pairs={{0,2},{1,3},{2,0},{3,1},{4,6},{5,7},{6,4},{7,5},{8,10},{9,11},{10,... | collective-permute-start | bytes 196616 | tf_op jit(solution)/shard_map/ppermute | solution.py:306
  10.1 2.6 %shard_map.40.l_ref = f32[128,2048]{1,0:T(8,128)S(1)} custom-call(bf16[128,2048]{1,0:T(8,128)(2,1)S(1)} %copy-done, bf16[128,2048]{1,0:T(8,128)(2,1)S(1)} %get-tuple-element.44.k_ref, bf16[128,2048]{1,0:T(8,128)(2,1)S(1)} %get-tuple-element.45.v_ref), custom_call_target="tpu_custom_call" | custom-call | flops 134217728 | bytes 1572864 | tf_op jit(solution)/shard_map/pallas_call | solution.py:18
  12.6 1.9 %collective-permute-done.4.refs_4_ = f32[128,128]{1,0:T(8,128)S(1)} collective-permute-done((f32[128,128]{1,0:T(8,128)S(1)}, f32[128,128]{1,0:T(8,128)S(1)}, u32[]{:S(2)}, u32[]{:S(2)}) %collective-permute-start.4) | collective-permute-done | bytes 65568 | tf_op jit(solution)/shard_map/ppermute | solution.py:306
  14.5 0.6 %collective-permute-done.2.refs_1_ = f32[2,128,128]{2,1,0:T(8,128)S(1)} collective-permute-done((f32[2,128,128]{2,1,0:T(8,128)S(1)}, f32[2,128,128]{2,1,0:T(8,128)S(1)}, u32[]{:S(2)}, u32[]{:S(2)}) %collective-permute-start.2) | collective-permute-done | bytes 131104 | tf_op jit(solution)/shard_map/ppermute | solution.py:306
  15.1 0.5 %collective-permute-start.5 = (f32[3,128,128]{2,1,0:T(8,128)S(1)}, f32[3,128,128]{2,1,0:T(8,128)S(1)}, u32[]{:S(2)}, u32[]{:S(2)}) collective-permute-start(f32[3,128,128]{2,1,0:T(8,128)S(1)} %shard_map.41), channel_id=1, source_target_pairs={{0,1},{1,0},{2,3},{3,2},{4,5},{5,4},{6,7},{7,6},{8,9},{9,8},{10,11... | collective-permute-start | bytes 589832 | tf_op jit(solution)/shard_map/ppermute | solution.py:301
  15.6 1.1 %collective-permute-done.5.refs_3_ = f32[3,128,128]{2,1,0:T(8,128)S(1)} collective-permute-done((f32[3,128,128]{2,1,0:T(8,128)S(1)}, f32[3,128,128]{2,1,0:T(8,128)S(1)}, u32[]{:S(2)}, u32[]{:S(2)}) %collective-permute-start.5) | collective-permute-done | bytes 196640 | tf_op jit(solution)/shard_map/ppermute | solution.py:301
  16.7 0.4 %collective-permute-start.7 = (f32[5,128,128]{2,1,0:T(8,128)S(1)}, f32[5,128,128]{2,1,0:T(8,128)S(1)}, u32[]{:S(2)}, u32[]{:S(2)}) collective-permute-start(f32[5,128,128]{2,1,0:T(8,128)S(1)} %get-tuple-element.59), channel_id=1, source_target_pairs={{0,1},{1,0},{2,3},{3,2},{4,5},{5,4},{6,7},{7,6},{8,9},{9,8},{10,11... | collective-permute-start | bytes 983048 | tf_op jit(solution)/shard_map/ppermute | solution.py:301
  17.2 2.6 %collective-permute-start.6 = (f32[128,128]{1,0:T(8,128)S(1)}, f32[128,128]{1,0:T(8,128)S(1)}, u32[]{:S(2)}, u32[]{:S(2)}) collective-permute-start(f32[128,128]{1,0:T(8,128)S(1)} %get-tuple-element.58), channel_id=1, source_target_pairs={{0,16},{2,18},{4,20},{6,22},{8,24},{10,26},{12,28},{14,30},{16,0},... | collective-permute-start | bytes 196616 | tf_op jit(solution)/shard_map/ppermute | solution.py:335
  19.8 3.9 %collective-permute-done.6.e_ref = f32[128,128]{1,0:T(8,128)S(1)} collective-permute-done((f32[128,128]{1,0:T(8,128)S(1)}, f32[128,128]{1,0:T(8,128)S(1)}, u32[]{:S(2)}, u32[]{:S(2)}) %collective-permute-start.6) | collective-permute-done | bytes 65568 | tf_op jit(solution)/shard_map/ppermute | solution.py:335
  23.9 1.1 %collective-permute-done.8.o_ref = f32[128,128]{1,0:T(8,128)S(1)} collective-permute-done((f32[128,128]{1,0:T(8,128)S(1)}, f32[128,128]{1,0:T(8,128)S(1)}, u32[]{:S(2)}, u32[]{:S(2)}) %collective-permute-start.8) | collective-permute-done | bytes 65568 | tf_op jit(solution)/shard_map/ppermute | solution.py:301
  25.0 1.6 %collective-permute-start.9 = (f32[2,128,128]{2,1,0:T(8,128)S(1)}, f32[2,128,128]{2,1,0:T(8,128)S(1)}, u32[]{:S(2)}, u32[]{:S(2)}) collective-permute-start(f32[2,128,128]{2,1,0:T(8,128)S(1)} %get-tuple-element.73), channel_id=1, source_target_pairs={{0,12},{1,15},{2,14},{3,13},{4,8},{5,11},{6,10},{7,9},{8,4},{9,7},... | collective-permute-start | bytes 393224 | tf_op jit(solution)/shard_map/ppermute | solution.py:306
  26.6 1.3 %collective-permute-start.10 = (f32[2,128,128]{2,1,0:T(8,128)S(1)}, f32[2,128,128]{2,1,0:T(8,128)S(1)}, u32[]{:S(2)}, u32[]{:S(2)}) collective-permute-start(f32[2,128,128]{2,1,0:T(8,128)S(1)} %get-tuple-element.74), channel_id=1, source_target_pairs={{0,8},{1,11},{2,10},{3,9},{4,12},{5,15},{6,14},{7,13},{8,0},{9,3},... | collective-permute-start | bytes 393224 | tf_op jit(solution)/shard_map/ppermute | solution.py:306
  27.9 0.6 %collective-permute-start.11 = (f32[2,128,128]{2,1,0:T(8,128)S(1)}, f32[2,128,128]{2,1,0:T(8,128)S(1)}, u32[]{:S(2)}, u32[]{:S(2)}) collective-permute-start(f32[2,128,128]{2,1,0:T(8,128)S(1)} %get-tuple-element.75), channel_id=1, source_target_pairs={{0,4},{1,7},{2,6},{3,5},{4,0},{5,3},{6,2},{7,1},{8,12},{9,15},{10,... | collective-permute-start | bytes 393224 | tf_op jit(solution)/shard_map/ppermute | solution.py:306
  28.6 2.1 %collective-permute-start.12 = (f32[128,128]{1,0:T(8,128)S(1)}, f32[128,128]{1,0:T(8,128)S(1)}, u32[]{:S(2)}, u32[]{:S(2)}) collective-permute-start(f32[128,128]{1,0:T(8,128)S(1)} %get-tuple-element.76), channel_id=1, source_target_pairs={{0,2},{1,3},{2,0},{3,1},{4,6},{5,7},{6,4},{7,5},{8,10},{9,11},{10,... | collective-permute-start | bytes 196616 | tf_op jit(solution)/shard_map/ppermute | solution.py:306
  30.7 4.1 %collective-permute-done.12.refs_3_ = f32[128,128]{1,0:T(8,128)S(1)} collective-permute-done((f32[128,128]{1,0:T(8,128)S(1)}, f32[128,128]{1,0:T(8,128)S(1)}, u32[]{:S(2)}, u32[]{:S(2)}) %collective-permute-start.12) | collective-permute-done | bytes 65568 | tf_op jit(solution)/shard_map/ppermute | solution.py:306
  35.1 0.4 %collective-permute-start.13 = (f32[8,128,128]{2,1,0:T(8,128)S(1)}, f32[8,128,128]{2,1,0:T(8,128)S(1)}, u32[]{:S(2)}, u32[]{:S(2)}) collective-permute-start(f32[8,128,128]{2,1,0:T(8,128)S(1)} %shard_map.45), channel_id=1, source_target_pairs={{0,1},{1,0},{2,3},{3,2},{4,5},{5,4},{6,7},{7,6},{8,9},{9,8},{10,11... | collective-permute-start | bytes 1572872 | tf_op jit(solution)/shard_map/ppermute | solution.py:301
  35.6 0.4 %shard_map.46.d_ref = bf16[128,1024]{1,0:T(8,128)(2,1)S(1)} custom-call(bf16[128,2048]{1,0:T(8,128)(2,1)S(1)} %copy-done, f32[128,2048]{1,0:T(8,128)S(1)} %shard_map.40.l_ref, f32[8,128,128]{2,1,0:T(8,128)S(1)} %collective-permute-done.b_ref.g_ref, f32[2,128,128]{2,1,0:T(8,128)S(1)} %collective-permute-done.9.refs_0_, ...), custom_call_target="tpu_custom_call" | custom-call | flops 67108864 | bytes 2621440 | tf_op jit(solution)/shard_map/pallas_call | solution.py:18
  36.0 1.1 %collective-permute-done.13.c_ref = f32[8,128,128]{2,1,0:T(8,128)S(1)} collective-permute-done((f32[8,128,128]{2,1,0:T(8,128)S(1)}, f32[8,128,128]{2,1,0:T(8,128)S(1)}, u32[]{:S(2)}, u32[]{:S(2)}) %collective-permute-start.13) | collective-permute-done | bytes 524320 | tf_op jit(solution)/shard_map/ppermute | solution.py:301
  37.1 1.2 %shard_map.47 = bf16[128,2048]{1,0:T(8,128)(2,1)} custom-call(bf16[128,2048]{1,0:T(8,128)(2,1)S(1)} %copy-done, f32[128,2048]{1,0:T(8,128)S(1)} %shard_map.40.l_ref, f32[8,128,128]{2,1,0:T(8,128)S(1)} %collective-permute-done.13.c_ref, bf16[128,1024]{1,0:T(8,128)(2,1)S(1)} %shard_map.46.d_ref), custom_call_target="tpu_custom_call" | custom-call | flops 67108864 | bytes 2359296 | tf_op jit(solution)/shard_map/pallas_call | solution.py:18
  (17 shorter events, 1.1 us)
Async XLA Ops:
  1.5 2.1 %collective-permute-start = (f32[8,128,128]{2,1,0:T(8,128)S(1)}, f32[8,128,128]{2,1,0:T(8,128)S(1)}, u32[]{:S(2)}, u32[]{:S(2)}) collective-permute-start(f32[8,128,128]{2,1,0:T(8,128)S(1)} %get-tuple-element.46), channel_id=1, source_target_pairs={{0,1},{1,0},{2,3},{3,2},{4,5},{5,4},{6,7},{7,6},{8,9},{9,8},{10,11... | collective-permute-start | bytes 1572872 | tf_op jit(solution)/shard_map/ppermute | solution.py:301
  2.3 7.7 %copy-start = (bf16[128,2048]{1,0:T(8,128)(2,1)S(1)}, bf16[128,2048]{1,0:T(8,128)(2,1)}, u32[]{:S(2)}) copy-start(bf16[128,2048]{1,0:T(8,128)(2,1)} %q_ref.4) | copy-start | bytes 1572868
  3.6 10.8 %collective-permute-start.1 = (f32[2,128,128]{2,1,0:T(8,128)S(1)}, f32[2,128,128]{2,1,0:T(8,128)S(1)}, u32[]{:S(2)}, u32[]{:S(2)}) collective-permute-start(f32[2,128,128]{2,1,0:T(8,128)S(1)} %get-tuple-element.47), channel_id=1, source_target_pairs={{0,12},{1,15},{2,14},{3,13},{4,8},{5,11},{6,10},{7,9},{8,4},{9,7},... | collective-permute-start | bytes 393224 | tf_op jit(solution)/shard_map/ppermute | solution.py:306
  7.6 7.5 %collective-permute-start.2 = (f32[2,128,128]{2,1,0:T(8,128)S(1)}, f32[2,128,128]{2,1,0:T(8,128)S(1)}, u32[]{:S(2)}, u32[]{:S(2)}) collective-permute-start(f32[2,128,128]{2,1,0:T(8,128)S(1)} %get-tuple-element.48), channel_id=1, source_target_pairs={{0,8},{1,11},{2,10},{3,9},{4,12},{5,15},{6,14},{7,13},{8,0},{9,3},... | collective-permute-start | bytes 393224 | tf_op jit(solution)/shard_map/ppermute | solution.py:306
  8.0 7.1 %collective-permute-start.3 = (f32[2,128,128]{2,1,0:T(8,128)S(1)}, f32[2,128,128]{2,1,0:T(8,128)S(1)}, u32[]{:S(2)}, u32[]{:S(2)}) collective-permute-start(f32[2,128,128]{2,1,0:T(8,128)S(1)} %get-tuple-element.49), channel_id=1, source_target_pairs={{0,4},{1,7},{2,6},{3,5},{4,0},{5,3},{6,2},{7,1},{8,12},{9,15},{10,... | collective-permute-start | bytes 393224 | tf_op jit(solution)/shard_map/ppermute | solution.py:306
  8.2 6.2 %collective-permute-start.4 = (f32[128,128]{1,0:T(8,128)S(1)}, f32[128,128]{1,0:T(8,128)S(1)}, u32[]{:S(2)}, u32[]{:S(2)}) collective-permute-start(f32[128,128]{1,0:T(8,128)S(1)} %get-tuple-element.50), channel_id=1, source_target_pairs={{0,2},{1,3},{2,0},{3,1},{4,6},{5,7},{6,4},{7,5},{8,10},{9,11},{10,... | collective-permute-start | bytes 196616 | tf_op jit(solution)/shard_map/ppermute | solution.py:306
  15.1 1.6 %collective-permute-start.5 = (f32[3,128,128]{2,1,0:T(8,128)S(1)}, f32[3,128,128]{2,1,0:T(8,128)S(1)}, u32[]{:S(2)}, u32[]{:S(2)}) collective-permute-start(f32[3,128,128]{2,1,0:T(8,128)S(1)} %shard_map.41), channel_id=1, source_target_pairs={{0,1},{1,0},{2,3},{3,2},{4,5},{5,4},{6,7},{7,6},{8,9},{9,8},{10,11... | collective-permute-start | bytes 589832 | tf_op jit(solution)/shard_map/ppermute | solution.py:301
  16.7 7.0 %collective-permute-start.7 = (f32[5,128,128]{2,1,0:T(8,128)S(1)}, f32[5,128,128]{2,1,0:T(8,128)S(1)}, u32[]{:S(2)}, u32[]{:S(2)}) collective-permute-start(f32[5,128,128]{2,1,0:T(8,128)S(1)} %get-tuple-element.59), channel_id=1, source_target_pairs={{0,1},{1,0},{2,3},{3,2},{4,5},{5,4},{6,7},{7,6},{8,9},{9,8},{10,11... | collective-permute-start | bytes 983048 | tf_op jit(solution)/shard_map/ppermute | solution.py:301
  17.2 6.6 %collective-permute-start.6 = (f32[128,128]{1,0:T(8,128)S(1)}, f32[128,128]{1,0:T(8,128)S(1)}, u32[]{:S(2)}, u32[]{:S(2)}) collective-permute-start(f32[128,128]{1,0:T(8,128)S(1)} %get-tuple-element.58), channel_id=1, source_target_pairs={{0,16},{2,18},{4,20},{6,22},{8,24},{10,26},{12,28},{14,30},{16,0},... | collective-permute-start | bytes 196616 | tf_op jit(solution)/shard_map/ppermute | solution.py:335
  23.7 1.3 %collective-permute-start.8 = (f32[128,128]{1,0:T(8,128)S(1)}, f32[128,128]{1,0:T(8,128)S(1)}, u32[]{:S(2)}, u32[]{:S(2)}) collective-permute-start(f32[128,128]{1,0:T(8,128)S(1)} %collective-permute-done.6.e_ref), channel_id=1, source_target_pairs={{0,1},{1,0},{2,3},{3,2},{4,5},{5,4},{6,7},{7,6},{8,9},{9,8},{10,11... | collective-permute-start | bytes 196616 | tf_op jit(solution)/shard_map/ppermute | solution.py:301
  25.0 9.7 %collective-permute-start.9 = (f32[2,128,128]{2,1,0:T(8,128)S(1)}, f32[2,128,128]{2,1,0:T(8,128)S(1)}, u32[]{:S(2)}, u32[]{:S(2)}) collective-permute-start(f32[2,128,128]{2,1,0:T(8,128)S(1)} %get-tuple-element.73), channel_id=1, source_target_pairs={{0,12},{1,15},{2,14},{3,13},{4,8},{5,11},{6,10},{7,9},{8,4},{9,7},... | collective-permute-start | bytes 393224 | tf_op jit(solution)/shard_map/ppermute | solution.py:306
  26.6 8.4 %collective-permute-start.10 = (f32[2,128,128]{2,1,0:T(8,128)S(1)}, f32[2,128,128]{2,1,0:T(8,128)S(1)}, u32[]{:S(2)}, u32[]{:S(2)}) collective-permute-start(f32[2,128,128]{2,1,0:T(8,128)S(1)} %get-tuple-element.74), channel_id=1, source_target_pairs={{0,8},{1,11},{2,10},{3,9},{4,12},{5,15},{6,14},{7,13},{8,0},{9,3},... | collective-permute-start | bytes 393224 | tf_op jit(solution)/shard_map/ppermute | solution.py:306
  27.9 7.1 %collective-permute-start.11 = (f32[2,128,128]{2,1,0:T(8,128)S(1)}, f32[2,128,128]{2,1,0:T(8,128)S(1)}, u32[]{:S(2)}, u32[]{:S(2)}) collective-permute-start(f32[2,128,128]{2,1,0:T(8,128)S(1)} %get-tuple-element.75), channel_id=1, source_target_pairs={{0,4},{1,7},{2,6},{3,5},{4,0},{5,3},{6,2},{7,1},{8,12},{9,15},{10,... | collective-permute-start | bytes 393224 | tf_op jit(solution)/shard_map/ppermute | solution.py:306
  28.6 6.1 %collective-permute-start.12 = (f32[128,128]{1,0:T(8,128)S(1)}, f32[128,128]{1,0:T(8,128)S(1)}, u32[]{:S(2)}, u32[]{:S(2)}) collective-permute-start(f32[128,128]{1,0:T(8,128)S(1)} %get-tuple-element.76), channel_id=1, source_target_pairs={{0,2},{1,3},{2,0},{3,1},{4,6},{5,7},{6,4},{7,5},{8,10},{9,11},{10,... | collective-permute-start | bytes 196616 | tf_op jit(solution)/shard_map/ppermute | solution.py:306
  35.1 2.0 %collective-permute-start.13 = (f32[8,128,128]{2,1,0:T(8,128)S(1)}, f32[8,128,128]{2,1,0:T(8,128)S(1)}, u32[]{:S(2)}, u32[]{:S(2)}) collective-permute-start(f32[8,128,128]{2,1,0:T(8,128)S(1)} %shard_map.45), channel_id=1, source_target_pairs={{0,1},{1,0},{2,3},{3,2},{4,5},{5,4},{6,7},{7,6},{8,9},{9,8},{10,11... | collective-permute-start | bytes 1572872 | tf_op jit(solution)/shard_map/ppermute | solution.py:301

commit v5 on v4

--- a/solution.py
+++ b/solution.py
@@ -13,7 +13,7 @@
 LIMIT = 8 * 1024 * 1024
 
 
-def call(kernel, outs, args, flops=0, ins=None, out_specs=None, scratch=()):
+def call(kernel, outs, args, flops=0, ins=None, out_specs=None, scratch=(), aliases={}):
     moved = sum(a.size * a.dtype.itemsize for a in args)
     return pl.pallas_call(
         kernel,
@@ -21,6 +21,7 @@
         in_specs=ins or [VMEM] * len(args),
         out_specs=out_specs or ([VMEM] * len(outs) if isinstance(outs, list) else VMEM),
         scratch_shapes=scratch,
+        input_output_aliases=aliases,
         compiler_params=pltpu.CompilerParams(vmem_limit_bytes=LIMIT),
         cost_estimate=pl.CostEstimate(flops=flops, bytes_accessed=moved, transcendentals=0),
     )(*args)
@@ -65,10 +66,13 @@
             for i, (src, dst) in enumerate(((k_hbm, k_ref), (v_hbm, v_ref))):
                 copies.append(pltpu.make_async_copy(src.at[:, cols], dst.at[:, cols], sems.at[n, i]))
                 copies[-1].start()
-        for copy in copies:
-            copy.wait()
-        for n, h in enumerate(heads_of(1 - lax.axis_index("narrow"), place_in_cube(group), group)):
-            s_ref[n] = state(k_ref[:, head(h)], v_ref[:, head(h)])
+        heads = heads_of(1 - lax.axis_index("narrow"), place_in_cube(group), group)
+        lower = [2 * turn for turn in range(turns_of(group))]
+        for n in range(2):
+            copies[2 * n].wait()
+            copies[2 * n + 1].wait()
+            for m in lower if n == 0 else [m for m in range(group) if m not in lower]:
+                s_ref[m] = state(k_ref[:, head(heads[m])], v_ref[:, head(heads[m])])
 
     return call(
         kernel,
@@ -135,11 +139,11 @@
         core = lax.axis_index("narrow")
         for n, h in enumerate(heads_of(core, place_in_cube(group), group)):
             carry = piece(refs, n, turns) + jnp.where(core == 1, g_ref[n], 0.0)
-            o_ref[:, n * HEAD_DIM : (n + 1) * HEAD_DIM] = attended(q_ref[:, head(h)], l_ref[:, head(h)], carry)
+            o_ref[:, head(h)] = attended(q_ref[:, head(h)], l_ref[:, head(h)], carry)
 
     return call(
         kernel,
-        pltpu.VMEM((tokens, group * HEAD_DIM), jnp.bfloat16),
+        pltpu.VMEM(queries.shape, jnp.bfloat16),
         (queries, local, got, *pieces),
         4 * group * tokens * HEAD_DIM * HEAD_DIM,
     )
@@ -150,9 +154,8 @@
     rows = tokens // parts
 
     def kernel(q_ref, l_ref, c_ref, d_ref, o_hbm, y_ref, sems):
+        del d_ref
         core, place = lax.axis_index("narrow"), place_in_cube(group)
-        for n, h in enumerate(heads_of(core, place, group)):
-            y_ref[:, head(h)] = d_ref[:, n * HEAD_DIM : (n + 1) * HEAD_DIM]
         copies = []
         for p in range(parts):
             some = slice(p * rows, (p + 1) * rows)
@@ -165,12 +168,13 @@
 
     return call(
         kernel,
-        jax.ShapeDtypeStruct(queries.shape, jnp.bfloat16),
+        [jax.ShapeDtypeStruct(queries.shape, jnp.bfloat16), pltpu.VMEM(queries.shape, jnp.bfloat16)],
         (queries, local, carry, done),
         4 * group * tokens * HEAD_DIM * HEAD_DIM,
-        out_specs=HBM,
-        scratch=[pltpu.VMEM(queries.shape, jnp.bfloat16), pltpu.SemaphoreType.DMA((parts,))],
-    )
+        out_specs=[HBM, VMEM],
+        scratch=[pltpu.SemaphoreType.DMA((parts,))],
+        aliases={3: 1},
+    )[0]
 
 
 def piece(refs, n, turns):
@@ -330,15 +334,22 @@
     running, lacking = gathered(pairs, swapped, near, mine)
     cube = lax.axis_index("wide") // group
     earlier = jnp.zeros_like(running) if groups != 2 else None
+    crossed = 1 if groups == 2 else 0
     step = 1
     while step < groups:
-        seen = lax.ppermute(running, "wide", [(i, i ^ (step * group)) for i in range(chips)])
+        seen = lax.ppermute(
+            running,
+            ("wide", "narrow"),
+            [(i * cores + c, (i ^ (step * group)) * cores + (c ^ crossed)) for i in range(chips) for c in range(cores)],
+        )
         earlier = seen if groups == 2 else earlier + jnp.where((cube & step) != 0, seen, 0.0)
         running = running + seen
         step *= 2
     received = swap_cores(lacking)
     earlier, received = lax.optimization_barrier((earlier, received))
     others = swap_cores(earlier)
+    if crossed:
+        earlier, others = others, earlier
     pieces = cube_prefixes(pairs, swapped, near, mine, received, group)
     others, *pieces = lax.optimization_barrier((others, *pieces))
     *pairs, far, mine = add_earlier(pieces, earlier, others, groups == 2, group)

time: 38.4 us -> 38.2 us (level)
    ppermute x5, starting transfers between devices: 1.89 us -> 2.3 us  [swap_cores(): return lax.ppermute(block, 'narrow', [(0, 1), (1, 0)])]
  transfers between devices with their start and end apart: 14 -> 14, of which waited for: 9 -> 8; matrix products, arithmetic and copies ran while one was open for 0% -> 0% of each run, Pallas kernels for 9% -> 9%
where the time goes in v5:
time: 38.2 us; the launch traced here: 38.1 us
  starting transfers between devices  16.7 us (44%)
  waiting for transfers between devices  15 us (39%)
  Pallas kernels  6.31 us (17%)
    ppermute x8, starting transfers between devices, pair_chips(): return lax.ppermute(block, ('wide', 'narrow'), route)  12.1 us
    ppermute x8, waiting for transfers between devices, pair_chips(): return lax.ppermute(block, ('wide', 'narrow'), route)  6.56 us
    pallas_call x11, Pallas kernels, call(): pl.pallas_call(kernel, out_shape=outs, in_specs=ins or [VMEM] * len(args)...  6.31 us
    ppermute x5, waiting for transfers between devices, swap_cores(): return lax.ppermute(block, 'narrow', [(0, 1), (1, 0)])  4.42 us
    ppermute x1, waiting for transfers between devices, shards(): lax.ppermute(running, ('wide', 'narrow'), [(i * cores + c, (i ^ step * gr...  4 us
    ppermute x1, starting transfers between devices, shards(): lax.ppermute(running, ('wide', 'narrow'), [(i * cores + c, (i ^ step * gr...  2.38 us
    ppermute x5, starting transfers between devices, swap_cores(): return lax.ppermute(block, 'narrow', [(0, 1), (1, 0)])  2.3 us
  transfers between devices with their start and end apart: 14, of which 8 were waited for; matrix products, arithmetic and copies ran while one was open for 0% of the time, Pallas kernels for 9%

profile of v5, /device:TPU:0, one launch (start us, length us, event | category | flops | bytes accessed | tf_op | source)
XLA Modules:
  0.0 38.1 jit_solution(5893145545694392992)
XLA Ops:
  0.0 1.5 %shard_map.37 = (f32[8,128,128]{2,1,0:T(8,128)S(1)}, bf16[128,2048]{1,0:T(8,128)(2,1)S(1)}, bf16[128,2048]{1,0:T(8,128)(2,1)S(1)}) custom-call(bf16[128,2048]{1,0:T(8,128)(2,1)} %k_hbm.1, bf16[128,2048]{1,0:T(8,128)(2,1)} %v_hbm.1), custom_call_target="tpu_custom_call" | custom-call | flops 33554432 | bytes 1048576 | tf_op jit(solution)/shard_map/pallas_call | solution.py:18
  1.6 0.5 %collective-permute-start = (f32[8,128,128]{2,1,0:T(8,128)S(1)}, f32[8,128,128]{2,1,0:T(8,128)S(1)}, u32[]{:S(2)}, u32[]{:S(2)}) collective-permute-start(f32[8,128,128]{2,1,0:T(8,128)S(1)} %get-tuple-element.47), channel_id=1, source_target_pairs={{0,1},{1,0},{2,3},{3,2},{4,5},{5,4},{6,7},{7,6},{8,9},{9,8},{10,11... | collective-permute-start | bytes 1572872 | tf_op jit(solution)/shard_map/ppermute | solution.py:305
  2.4 1.2 %collective-permute-done.b_ref.g_ref = f32[8,128,128]{2,1,0:T(8,128)S(1)} collective-permute-done((f32[8,128,128]{2,1,0:T(8,128)S(1)}, f32[8,128,128]{2,1,0:T(8,128)S(1)}, u32[]{:S(2)}, u32[]{:S(2)}) %collective-permute-start) | collective-permute-done | bytes 524320 | tf_op jit(solution)/shard_map/ppermute | solution.py:305
  3.7 4.0 %collective-permute-start.1 = (f32[2,128,128]{2,1,0:T(8,128)S(1)}, f32[2,128,128]{2,1,0:T(8,128)S(1)}, u32[]{:S(2)}, u32[]{:S(2)}) collective-permute-start(f32[2,128,128]{2,1,0:T(8,128)S(1)} %get-tuple-element.48), channel_id=1, source_target_pairs={{0,12},{1,15},{2,14},{3,13},{4,8},{5,11},{6,10},{7,9},{8,4},{9,7},... | collective-permute-start | bytes 393224 | tf_op jit(solution)/shard_map/ppermute | solution.py:310
  7.6 0.5 %collective-permute-start.2 = (f32[2,128,128]{2,1,0:T(8,128)S(1)}, f32[2,128,128]{2,1,0:T(8,128)S(1)}, u32[]{:S(2)}, u32[]{:S(2)}) collective-permute-start(f32[2,128,128]{2,1,0:T(8,128)S(1)} %get-tuple-element.49), channel_id=1, source_target_pairs={{0,8},{1,11},{2,10},{3,9},{4,12},{5,15},{6,14},{7,13},{8,0},{9,3},... | collective-permute-start | bytes 393224 | tf_op jit(solution)/shard_map/ppermute | solution.py:310
  8.3 1.8 %collective-permute-start.4 = (f32[128,128]{1,0:T(8,128)S(1)}, f32[128,128]{1,0:T(8,128)S(1)}, u32[]{:S(2)}, u32[]{:S(2)}) collective-permute-start(f32[128,128]{1,0:T(8,128)S(1)} %get-tuple-element.51), channel_id=1, source_target_pairs={{0,2},{1,3},{2,0},{3,1},{4,6},{5,7},{6,4},{7,5},{8,10},{9,11},{10,... | collective-permute-start | bytes 196616 | tf_op jit(solution)/shard_map/ppermute | solution.py:310
  10.1 2.6 %shard_map.40.l_ref = f32[128,2048]{1,0:T(8,128)S(1)} custom-call(bf16[128,2048]{1,0:T(8,128)(2,1)S(1)} %copy-done, bf16[128,2048]{1,0:T(8,128)(2,1)S(1)} %get-tuple-element.45.k_ref, bf16[128,2048]{1,0:T(8,128)(2,1)S(1)} %get-tuple-element.46.v_ref), custom_call_target="tpu_custom_call" | custom-call | flops 134217728 | bytes 1572864 | tf_op jit(solution)/shard_map/pallas_call | solution.py:18
  12.7 1.9 %collective-permute-done.4.refs_4_ = f32[128,128]{1,0:T(8,128)S(1)} collective-permute-done((f32[128,128]{1,0:T(8,128)S(1)}, f32[128,128]{1,0:T(8,128)S(1)}, u32[]{:S(2)}, u32[]{:S(2)}) %collective-permute-start.4) | collective-permute-done | bytes 65568 | tf_op jit(solution)/shard_map/ppermute | solution.py:310
  14.5 0.6 %collective-permute-done.2.refs_1_ = f32[2,128,128]{2,1,0:T(8,128)S(1)} collective-permute-done((f32[2,128,128]{2,1,0:T(8,128)S(1)}, f32[2,128,128]{2,1,0:T(8,128)S(1)}, u32[]{:S(2)}, u32[]{:S(2)}) %collective-permute-start.2) | collective-permute-done | bytes 131104 | tf_op jit(solution)/shard_map/ppermute | solution.py:310
  15.2 0.5 %collective-permute-start.5 = (f32[3,128,128]{2,1,0:T(8,128)S(1)}, f32[3,128,128]{2,1,0:T(8,128)S(1)}, u32[]{:S(2)}, u32[]{:S(2)}) collective-permute-start(f32[3,128,128]{2,1,0:T(8,128)S(1)} %shard_map.41), channel_id=1, source_target_pairs={{0,1},{1,0},{2,3},{3,2},{4,5},{5,4},{6,7},{7,6},{8,9},{9,8},{10,11... | collective-permute-start | bytes 589832 | tf_op jit(solution)/shard_map/ppermute | solution.py:305
  15.6 1.1 %collective-permute-done.5.refs_3_ = f32[3,128,128]{2,1,0:T(8,128)S(1)} collective-permute-done((f32[3,128,128]{2,1,0:T(8,128)S(1)}, f32[3,128,128]{2,1,0:T(8,128)S(1)}, u32[]{:S(2)}, u32[]{:S(2)}) %collective-permute-start.5) | collective-permute-done | bytes 196640 | tf_op jit(solution)/shard_map/ppermute | solution.py:305
  16.8 0.4 %collective-permute-start.7 = (f32[5,128,128]{2,1,0:T(8,128)S(1)}, f32[5,128,128]{2,1,0:T(8,128)S(1)}, u32[]{:S(2)}, u32[]{:S(2)}) collective-permute-start(f32[5,128,128]{2,1,0:T(8,128)S(1)} %get-tuple-element.60), channel_id=1, source_target_pairs={{0,1},{1,0},{2,3},{3,2},{4,5},{5,4},{6,7},{7,6},{8,9},{9,8},{10,11... | collective-permute-start | bytes 983048 | tf_op jit(solution)/shard_map/ppermute | solution.py:305
  17.2 2.4 %collective-permute-start.6 = (f32[128,128]{1,0:T(8,128)S(1)}, f32[128,128]{1,0:T(8,128)S(1)}, u32[]{:S(2)}, u32[]{:S(2)}) collective-permute-start(f32[128,128]{1,0:T(8,128)S(1)} %get-tuple-element.59), channel_id=1, source_target_pairs={{0,17},{1,16},{2,19},{3,18},{4,21},{5,20},{6,23},{7,22},{8,25},{9,... | collective-permute-start | bytes 196616 | tf_op jit(solution)/shard_map/ppermute | solution.py:340
  19.6 4.0 %collective-permute-done.6.o_ref = f32[128,128]{1,0:T(8,128)S(1)} collective-permute-done((f32[128,128]{1,0:T(8,128)S(1)}, f32[128,128]{1,0:T(8,128)S(1)}, u32[]{:S(2)}, u32[]{:S(2)}) %collective-permute-start.6) | collective-permute-done | bytes 65568 | tf_op jit(solution)/shard_map/ppermute | solution.py:340
  23.9 1.0 %collective-permute-done.8.e_ref = f32[128,128]{1,0:T(8,128)S(1)} collective-permute-done((f32[128,128]{1,0:T(8,128)S(1)}, f32[128,128]{1,0:T(8,128)S(1)}, u32[]{:S(2)}, u32[]{:S(2)}) %collective-permute-start.8) | collective-permute-done | bytes 65568 | tf_op jit(solution)/shard_map/ppermute | solution.py:305
  24.9 1.8 %collective-permute-start.9 = (f32[2,128,128]{2,1,0:T(8,128)S(1)}, f32[2,128,128]{2,1,0:T(8,128)S(1)}, u32[]{:S(2)}, u32[]{:S(2)}) collective-permute-start(f32[2,128,128]{2,1,0:T(8,128)S(1)} %get-tuple-element.74), channel_id=1, source_target_pairs={{0,12},{1,15},{2,14},{3,13},{4,8},{5,11},{6,10},{7,9},{8,4},{9,7},... | collective-permute-start | bytes 393224 | tf_op jit(solution)/shard_map/ppermute | solution.py:310
  26.7 0.8 %collective-permute-start.10 = (f32[2,128,128]{2,1,0:T(8,128)S(1)}, f32[2,128,128]{2,1,0:T(8,128)S(1)}, u32[]{:S(2)}, u32[]{:S(2)}) collective-permute-start(f32[2,128,128]{2,1,0:T(8,128)S(1)} %get-tuple-element.75), channel_id=1, source_target_pairs={{0,8},{1,11},{2,10},{3,9},{4,12},{5,15},{6,14},{7,13},{8,0},{9,3},... | collective-permute-start | bytes 393224 | tf_op jit(solution)/shard_map/ppermute | solution.py:310
  27.5 0.9 %collective-permute-start.11 = (f32[2,128,128]{2,1,0:T(8,128)S(1)}, f32[2,128,128]{2,1,0:T(8,128)S(1)}, u32[]{:S(2)}, u32[]{:S(2)}) collective-permute-start(f32[2,128,128]{2,1,0:T(8,128)S(1)} %get-tuple-element.76), channel_id=1, source_target_pairs={{0,4},{1,7},{2,6},{3,5},{4,0},{5,3},{6,2},{7,1},{8,12},{9,15},{10,... | collective-permute-start | bytes 393224 | tf_op jit(solution)/shard_map/ppermute | solution.py:310
  28.4 2.1 %collective-permute-start.12 = (f32[128,128]{1,0:T(8,128)S(1)}, f32[128,128]{1,0:T(8,128)S(1)}, u32[]{:S(2)}, u32[]{:S(2)}) collective-permute-start(f32[128,128]{1,0:T(8,128)S(1)} %get-tuple-element.77), channel_id=1, source_target_pairs={{0,2},{1,3},{2,0},{3,1},{4,6},{5,7},{6,4},{7,5},{8,10},{9,11},{10,... | collective-permute-start | bytes 196616 | tf_op jit(solution)/shard_map/ppermute | solution.py:310
  30.5 4.1 %collective-permute-done.12.refs_3_ = f32[128,128]{1,0:T(8,128)S(1)} collective-permute-done((f32[128,128]{1,0:T(8,128)S(1)}, f32[128,128]{1,0:T(8,128)S(1)}, u32[]{:S(2)}, u32[]{:S(2)}) %collective-permute-start.12) | collective-permute-done | bytes 65568 | tf_op jit(solution)/shard_map/ppermute | solution.py:310
  34.7 0.7 %collective-permute-start.13 = (f32[8,128,128]{2,1,0:T(8,128)S(1)}, f32[8,128,128]{2,1,0:T(8,128)S(1)}, u32[]{:S(2)}, u32[]{:S(2)}) collective-permute-start(f32[8,128,128]{2,1,0:T(8,128)S(1)} %shard_map.45), channel_id=1, source_target_pairs={{0,1},{1,0},{2,3},{3,2},{4,5},{5,4},{6,7},{7,6},{8,9},{9,8},{10,11... | collective-permute-start | bytes 1572872 | tf_op jit(solution)/shard_map/ppermute | solution.py:305
  35.4 0.4 %shard_map.46.d_ref = bf16[128,2048]{1,0:T(8,128)(2,1)S(1)} custom-call(bf16[128,2048]{1,0:T(8,128)(2,1)S(1)} %copy-done, f32[128,2048]{1,0:T(8,128)S(1)} %shard_map.40.l_ref, f32[8,128,128]{2,1,0:T(8,128)S(1)} %collective-permute-done.b_ref.g_ref, f32[2,128,128]{2,1,0:T(8,128)S(1)} %collective-permute-done.9.refs_0_, ...), custom_call_target="tpu_custom_call" | custom-call | flops 67108864 | bytes 2621440 | tf_op jit(solution)/shard_map/pallas_call | solution.py:18
  35.8 1.1 %collective-permute-done.13.c_ref = f32[8,128,128]{2,1,0:T(8,128)S(1)} collective-permute-done((f32[8,128,128]{2,1,0:T(8,128)S(1)}, f32[8,128,128]{2,1,0:T(8,128)S(1)}, u32[]{:S(2)}, u32[]{:S(2)}) %collective-permute-start.13) | collective-permute-done | bytes 524320 | tf_op jit(solution)/shard_map/ppermute | solution.py:305
  37.0 1.1 %shard_map.47 = (bf16[128,2048]{1,0:T(8,128)(2,1)}, bf16[128,2048]{1,0:T(8,128)(2,1)S(1)}) custom-call(bf16[128,2048]{1,0:T(8,128)(2,1)S(1)} %copy-done, f32[128,2048]{1,0:T(8,128)S(1)} %shard_map.40.l_ref, f32[8,128,128]{2,1,0:T(8,128)S(1)} %collective-permute-done.13.c_ref, bf16[128,2048]{1,0:T(8,128)(2,1)S(1)} %shard_map.46.d_ref), custom_call_target="tpu_custom_call", output_to_operand_aliasing={{1}: (3, {})} | custom-call | flops 67108864 | bytes 2621440 | tf_op jit(solution)/shard_map/pallas_call | solution.py:18
  (17 shorter events, 1.0 us)
Async XLA Ops:
  1.6 2.1 %collective-permute-start = (f32[8,128,128]{2,1,0:T(8,128)S(1)}, f32[8,128,128]{2,1,0:T(8,128)S(1)}, u32[]{:S(2)}, u32[]{:S(2)}) collective-permute-start(f32[8,128,128]{2,1,0:T(8,128)S(1)} %get-tuple-element.47), channel_id=1, source_target_pairs={{0,1},{1,0},{2,3},{3,2},{4,5},{5,4},{6,7},{7,6},{8,9},{9,8},{10,11... | collective-permute-start | bytes 1572872 | tf_op jit(solution)/shard_map/ppermute | solution.py:305
  2.4 7.7 %copy-start = (bf16[128,2048]{1,0:T(8,128)(2,1)S(1)}, bf16[128,2048]{1,0:T(8,128)(2,1)}, u32[]{:S(2)}) copy-start(bf16[128,2048]{1,0:T(8,128)(2,1)} %q_ref.4) | copy-start | bytes 1572868
  3.7 10.8 %collective-permute-start.1 = (f32[2,128,128]{2,1,0:T(8,128)S(1)}, f32[2,128,128]{2,1,0:T(8,128)S(1)}, u32[]{:S(2)}, u32[]{:S(2)}) collective-permute-start(f32[2,128,128]{2,1,0:T(8,128)S(1)} %get-tuple-element.48), channel_id=1, source_target_pairs={{0,12},{1,15},{2,14},{3,13},{4,8},{5,11},{6,10},{7,9},{8,4},{9,7},... | collective-permute-start | bytes 393224 | tf_op jit(solution)/shard_map/ppermute | solution.py:310
  7.6 7.5 %collective-permute-start.2 = (f32[2,128,128]{2,1,0:T(8,128)S(1)}, f32[2,128,128]{2,1,0:T(8,128)S(1)}, u32[]{:S(2)}, u32[]{:S(2)}) collective-permute-start(f32[2,128,128]{2,1,0:T(8,128)S(1)} %get-tuple-element.49), channel_id=1, source_target_pairs={{0,8},{1,11},{2,10},{3,9},{4,12},{5,15},{6,14},{7,13},{8,0},{9,3},... | collective-permute-start | bytes 393224 | tf_op jit(solution)/shard_map/ppermute | solution.py:310
  8.1 7.1 %collective-permute-start.3 = (f32[2,128,128]{2,1,0:T(8,128)S(1)}, f32[2,128,128]{2,1,0:T(8,128)S(1)}, u32[]{:S(2)}, u32[]{:S(2)}) collective-permute-start(f32[2,128,128]{2,1,0:T(8,128)S(1)} %get-tuple-element.50), channel_id=1, source_target_pairs={{0,4},{1,7},{2,6},{3,5},{4,0},{5,3},{6,2},{7,1},{8,12},{9,15},{10,... | collective-permute-start | bytes 393224 | tf_op jit(solution)/shard_map/ppermute | solution.py:310
  8.3 6.2 %collective-permute-start.4 = (f32[128,128]{1,0:T(8,128)S(1)}, f32[128,128]{1,0:T(8,128)S(1)}, u32[]{:S(2)}, u32[]{:S(2)}) collective-permute-start(f32[128,128]{1,0:T(8,128)S(1)} %get-tuple-element.51), channel_id=1, source_target_pairs={{0,2},{1,3},{2,0},{3,1},{4,6},{5,7},{6,4},{7,5},{8,10},{9,11},{10,... | collective-permute-start | bytes 196616 | tf_op jit(solution)/shard_map/ppermute | solution.py:310
  15.2 1.5 %collective-permute-start.5 = (f32[3,128,128]{2,1,0:T(8,128)S(1)}, f32[3,128,128]{2,1,0:T(8,128)S(1)}, u32[]{:S(2)}, u32[]{:S(2)}) collective-permute-start(f32[3,128,128]{2,1,0:T(8,128)S(1)} %shard_map.41), channel_id=1, source_target_pairs={{0,1},{1,0},{2,3},{3,2},{4,5},{5,4},{6,7},{7,6},{8,9},{9,8},{10,11... | collective-permute-start | bytes 589832 | tf_op jit(solution)/shard_map/ppermute | solution.py:305
  16.8 6.8 %collective-permute-start.7 = (f32[5,128,128]{2,1,0:T(8,128)S(1)}, f32[5,128,128]{2,1,0:T(8,128)S(1)}, u32[]{:S(2)}, u32[]{:S(2)}) collective-permute-start(f32[5,128,128]{2,1,0:T(8,128)S(1)} %get-tuple-element.60), channel_id=1, source_target_pairs={{0,1},{1,0},{2,3},{3,2},{4,5},{5,4},{6,7},{7,6},{8,9},{9,8},{10,11... | collective-permute-start | bytes 983048 | tf_op jit(solution)/shard_map/ppermute | solution.py:305
  17.2 6.4 %collective-permute-start.6 = (f32[128,128]{1,0:T(8,128)S(1)}, f32[128,128]{1,0:T(8,128)S(1)}, u32[]{:S(2)}, u32[]{:S(2)}) collective-permute-start(f32[128,128]{1,0:T(8,128)S(1)} %get-tuple-element.59), channel_id=1, source_target_pairs={{0,17},{1,16},{2,19},{3,18},{4,21},{5,20},{6,23},{7,22},{8,25},{9,... | collective-permute-start | bytes 196616 | tf_op jit(solution)/shard_map/ppermute | solution.py:340
  23.6 1.3 %collective-permute-start.8 = (f32[128,128]{1,0:T(8,128)S(1)}, f32[128,128]{1,0:T(8,128)S(1)}, u32[]{:S(2)}, u32[]{:S(2)}) collective-permute-start(f32[128,128]{1,0:T(8,128)S(1)} %collective-permute-done.6.o_ref), channel_id=1, source_target_pairs={{0,1},{1,0},{2,3},{3,2},{4,5},{5,4},{6,7},{7,6},{8,9},{9,8},{10,11... | collective-permute-start | bytes 196616 | tf_op jit(solution)/shard_map/ppermute | solution.py:305
  24.9 9.7 %collective-permute-start.9 = (f32[2,128,128]{2,1,0:T(8,128)S(1)}, f32[2,128,128]{2,1,0:T(8,128)S(1)}, u32[]{:S(2)}, u32[]{:S(2)}) collective-permute-start(f32[2,128,128]{2,1,0:T(8,128)S(1)} %get-tuple-element.74), channel_id=1, source_target_pairs={{0,12},{1,15},{2,14},{3,13},{4,8},{5,11},{6,10},{7,9},{8,4},{9,7},... | collective-permute-start | bytes 393224 | tf_op jit(solution)/shard_map/ppermute | solution.py:310
  26.7 7.9 %collective-permute-start.10 = (f32[2,128,128]{2,1,0:T(8,128)S(1)}, f32[2,128,128]{2,1,0:T(8,128)S(1)}, u32[]{:S(2)}, u32[]{:S(2)}) collective-permute-start(f32[2,128,128]{2,1,0:T(8,128)S(1)} %get-tuple-element.75), channel_id=1, source_target_pairs={{0,8},{1,11},{2,10},{3,9},{4,12},{5,15},{6,14},{7,13},{8,0},{9,3},... | collective-permute-start | bytes 393224 | tf_op jit(solution)/shard_map/ppermute | solution.py:310
  27.5 7.1 %collective-permute-start.11 = (f32[2,128,128]{2,1,0:T(8,128)S(1)}, f32[2,128,128]{2,1,0:T(8,128)S(1)}, u32[]{:S(2)}, u32[]{:S(2)}) collective-permute-start(f32[2,128,128]{2,1,0:T(8,128)S(1)} %get-tuple-element.76), channel_id=1, source_target_pairs={{0,4},{1,7},{2,6},{3,5},{4,0},{5,3},{6,2},{7,1},{8,12},{9,15},{10,... | collective-permute-start | bytes 393224 | tf_op jit(solution)/shard_map/ppermute | solution.py:310
  28.4 6.2 %collective-permute-start.12 = (f32[128,128]{1,0:T(8,128)S(1)}, f32[128,128]{1,0:T(8,128)S(1)}, u32[]{:S(2)}, u32[]{:S(2)}) collective-permute-start(f32[128,128]{1,0:T(8,128)S(1)} %get-tuple-element.77), channel_id=1, source_target_pairs={{0,2},{1,3},{2,0},{3,1},{4,6},{5,7},{6,4},{7,5},{8,10},{9,11},{10,... | collective-permute-start | bytes 196616 | tf_op jit(solution)/shard_map/ppermute | solution.py:310
  34.7 2.3 %collective-permute-start.13 = (f32[8,128,128]{2,1,0:T(8,128)S(1)}, f32[8,128,128]{2,1,0:T(8,128)S(1)}, u32[]{:S(2)}, u32[]{:S(2)}) collective-permute-start(f32[8,128,128]{2,1,0:T(8,128)S(1)} %shard_map.45), channel_id=1, source_target_pairs={{0,1},{1,0},{2,3},{3,2},{4,5},{5,4},{6,7},{7,6},{8,9},{9,8},{10,11... | collective-permute-start | bytes 1572872 | tf_op jit(solution)/shard_map/ppermute | solution.py:305

commit v6 on v5

--- a/solution.py
+++ b/solution.py
@@ -9,7 +9,7 @@
 HEAD_DIM = 128
 VMEM = pl.BlockSpec(memory_space=pltpu.VMEM)
 HBM = pl.BlockSpec(memory_space=pltpu.HBM)
-NEAR = 1
+NEAR = HEADS // 4
 LIMIT = 8 * 1024 * 1024
 
 
@@ -40,7 +40,7 @@
 
 
 def partner(core, turn, group):
-    return (group - 2 * (turn + 1)) ^ (NEAR * core)
+    return (turn or group - 1) ^ (NEAR * core)
 
 
 def turns_of(group):

time: 38.2 us -> 38 us (level)
  waiting for transfers between devices: 15 us -> 14.4 us
    ppermute x1, waiting for transfers between devices: 4 us -> 2.31 us  [shards(): lax.ppermute(running, ('wide', 'narrow'), [(i * cores + c, (i ^ step * gr...]
    ppermute x8, waiting for transfers between devices: 6.56 us -> 7.78 us  [pair_chips(): return lax.ppermute(block, ('wide', 'narrow'), route)]
    ppermute x5, starting transfers between devices: 2.3 us -> 3.25 us  [swap_cores(): return lax.ppermute(block, 'narrow', [(0, 1), (1, 0)])]
    ppermute x8, starting transfers between devices: 12.1 us -> 11.1 us  [pair_chips(): return lax.ppermute(block, ('wide', 'narrow'), route)]
where the time goes in v6:
time: 38 us; the launch traced here: 37.9 us
  starting transfers between devices  17 us (45%)
  waiting for transfers between devices  14.4 us (38%)
  Pallas kernels  6.31 us (17%)
    ppermute x8, starting transfers between devices, pair_chips(): return lax.ppermute(block, ('wide', 'narrow'), route)  11.1 us
    ppermute x8, waiting for transfers between devices, pair_chips(): return lax.ppermute(block, ('wide', 'narrow'), route)  7.78 us
    pallas_call x11, Pallas kernels, call(): pl.pallas_call(kernel, out_shape=outs, in_specs=ins or [VMEM] * len(args)...  6.31 us
    ppermute x5, waiting for transfers between devices, swap_cores(): return lax.ppermute(block, 'narrow', [(0, 1), (1, 0)])  4.35 us
    ppermute x5, starting transfers between devices, swap_cores(): return lax.ppermute(block, 'narrow', [(0, 1), (1, 0)])  3.25 us
    ppermute x1, starting transfers between devices, shards(): lax.ppermute(running, ('wide', 'narrow'), [(i * cores + c, (i ^ step * gr...  2.68 us
    ppermute x1, waiting for transfers between devices, shards(): lax.ppermute(running, ('wide', 'narrow'), [(i * cores + c, (i ^ step * gr...  2.31 us
  transfers between devices with their start and end apart: 14, of which 8 were waited for; matrix products, arithmetic and copies ran while one was open for 0% of the time, Pallas kernels for 9%

profile of v6, /device:TPU:0, one launch (start us, length us, event | category | flops | bytes accessed | tf_op | source)
XLA Modules:
  0.0 37.9 jit_solution(7378871799812056058)
XLA Ops:
  0.0 1.5 %shard_map.37 = (f32[8,128,128]{2,1,0:T(8,128)S(1)}, bf16[128,2048]{1,0:T(8,128)(2,1)S(1)}, bf16[128,2048]{1,0:T(8,128)(2,1)S(1)}) custom-call(bf16[128,2048]{1,0:T(8,128)(2,1)} %k_hbm.1, bf16[128,2048]{1,0:T(8,128)(2,1)} %v_hbm.1), custom_call_target="tpu_custom_call" | custom-call | flops 33554432 | bytes 1048576 | tf_op jit(solution)/shard_map/pallas_call | solution.py:18
  1.6 0.5 %collective-permute-start = (f32[8,128,128]{2,1,0:T(8,128)S(1)}, f32[8,128,128]{2,1,0:T(8,128)S(1)}, u32[]{:S(2)}, u32[]{:S(2)}) collective-permute-start(f32[8,128,128]{2,1,0:T(8,128)S(1)} %get-tuple-element.47), channel_id=1, source_target_pairs={{0,1},{1,0},{2,3},{3,2},{4,5},{5,4},{6,7},{7,6},{8,9},{9,8},{10,11... | collective-permute-start | bytes 1572872 | tf_op jit(solution)/shard_map/ppermute | solution.py:305
  2.4 1.2 %collective-permute-done.b_ref.g_ref = f32[8,128,128]{2,1,0:T(8,128)S(1)} collective-permute-done((f32[8,128,128]{2,1,0:T(8,128)S(1)}, f32[8,128,128]{2,1,0:T(8,128)S(1)}, u32[]{:S(2)}, u32[]{:S(2)}) %collective-permute-start) | collective-permute-done | bytes 524320 | tf_op jit(solution)/shard_map/ppermute | solution.py:305
  3.7 4.9 %collective-permute-start.1 = (f32[2,128,128]{2,1,0:T(8,128)S(1)}, f32[2,128,128]{2,1,0:T(8,128)S(1)}, u32[]{:S(2)}, u32[]{:S(2)}) collective-permute-start(f32[2,128,128]{2,1,0:T(8,128)S(1)} %get-tuple-element.48), channel_id=1, source_target_pairs={{0,14},{1,7},{2,12},{3,5},{4,10},{5,3},{6,8},{7,1},{8,6},{9,15},{1... | collective-permute-start | bytes 393224 | tf_op jit(solution)/shard_map/ppermute | solution.py:310
  8.6 0.5 %collective-permute-start.2 = (f32[2,128,128]{2,1,0:T(8,128)S(1)}, f32[2,128,128]{2,1,0:T(8,128)S(1)}, u32[]{:S(2)}, u32[]{:S(2)}) collective-permute-start(f32[2,128,128]{2,1,0:T(8,128)S(1)} %get-tuple-element.49), channel_id=1, source_target_pairs={{0,2},{1,11},{2,0},{3,9},{4,6},{5,15},{6,4},{7,13},{8,10},{9,3},{1... | collective-permute-start | bytes 393224 | tf_op jit(solution)/shard_map/ppermute | solution.py:310
  9.1 0.5 %collective-permute-start.3 = (f32[2,128,128]{2,1,0:T(8,128)S(1)}, f32[2,128,128]{2,1,0:T(8,128)S(1)}, u32[]{:S(2)}, u32[]{:S(2)}) collective-permute-start(f32[2,128,128]{2,1,0:T(8,128)S(1)} %get-tuple-element.50), channel_id=1, source_target_pairs={{0,4},{1,13},{2,6},{3,15},{4,0},{5,9},{6,2},{7,11},{8,12},{9,5},{1... | collective-permute-start | bytes 393224 | tf_op jit(solution)/shard_map/ppermute | solution.py:310
  9.8 2.6 %shard_map.40.l_ref = f32[128,2048]{1,0:T(8,128)S(1)} custom-call(bf16[128,2048]{1,0:T(8,128)(2,1)S(1)} %copy-done, bf16[128,2048]{1,0:T(8,128)(2,1)S(1)} %get-tuple-element.45.k_ref, bf16[128,2048]{1,0:T(8,128)(2,1)S(1)} %get-tuple-element.46.v_ref), custom_call_target="tpu_custom_call" | custom-call | flops 134217728 | bytes 1572864 | tf_op jit(solution)/shard_map/pallas_call | solution.py:18
  12.3 2.4 %collective-permute-done.4.refs_4_ = f32[128,128]{1,0:T(8,128)S(1)} collective-permute-done((f32[128,128]{1,0:T(8,128)S(1)}, f32[128,128]{1,0:T(8,128)S(1)}, u32[]{:S(2)}, u32[]{:S(2)}) %collective-permute-start.4) | collective-permute-done | bytes 65568 | tf_op jit(solution)/shard_map/ppermute | solution.py:310
  14.8 0.5 %collective-permute-done.3.refs_2_ = f32[2,128,128]{2,1,0:T(8,128)S(1)} collective-permute-done((f32[2,128,128]{2,1,0:T(8,128)S(1)}, f32[2,128,128]{2,1,0:T(8,128)S(1)}, u32[]{:S(2)}, u32[]{:S(2)}) %collective-permute-start.3) | collective-permute-done | bytes 131104 | tf_op jit(solution)/shard_map/ppermute | solution.py:310
  15.3 0.3 collective-permute-start.5
  15.6 1.2 %collective-permute-done.5.refs_3_ = f32[3,128,128]{2,1,0:T(8,128)S(1)} collective-permute-done((f32[3,128,128]{2,1,0:T(8,128)S(1)}, f32[3,128,128]{2,1,0:T(8,128)S(1)}, u32[]{:S(2)}, u32[]{:S(2)}) %collective-permute-start.5) | collective-permute-done | bytes 196640 | tf_op jit(solution)/shard_map/ppermute | solution.py:305
  16.8 0.3 collective-permute-start.7
  17.1 2.7 %collective-permute-start.6 = (f32[128,128]{1,0:T(8,128)S(1)}, f32[128,128]{1,0:T(8,128)S(1)}, u32[]{:S(2)}, u32[]{:S(2)}) collective-permute-start(f32[128,128]{1,0:T(8,128)S(1)} %get-tuple-element.59), channel_id=1, source_target_pairs={{0,17},{1,16},{2,19},{3,18},{4,21},{5,20},{6,23},{7,22},{8,25},{9,... | collective-permute-start | bytes 196616 | tf_op jit(solution)/shard_map/ppermute | solution.py:340
  19.8 2.3 %collective-permute-done.6.o_ref = f32[128,128]{1,0:T(8,128)S(1)} collective-permute-done((f32[128,128]{1,0:T(8,128)S(1)}, f32[128,128]{1,0:T(8,128)S(1)}, u32[]{:S(2)}, u32[]{:S(2)}) %collective-permute-start.6) | collective-permute-done | bytes 65568 | tf_op jit(solution)/shard_map/ppermute | solution.py:340
  22.1 1.6 %collective-permute-start.8 = (f32[128,128]{1,0:T(8,128)S(1)}, f32[128,128]{1,0:T(8,128)S(1)}, u32[]{:S(2)}, u32[]{:S(2)}) collective-permute-start(f32[128,128]{1,0:T(8,128)S(1)} %collective-permute-done.6.o_ref), channel_id=1, source_target_pairs={{0,1},{1,0},{2,3},{3,2},{4,5},{5,4},{6,7},{7,6},{8,9},{9,8},{10,11... | collective-permute-start | bytes 196616 | tf_op jit(solution)/shard_map/ppermute | solution.py:305
  23.8 0.8 %collective-permute-done.8.e_ref = f32[128,128]{1,0:T(8,128)S(1)} collective-permute-done((f32[128,128]{1,0:T(8,128)S(1)}, f32[128,128]{1,0:T(8,128)S(1)}, u32[]{:S(2)}, u32[]{:S(2)}) %collective-permute-start.8) | collective-permute-done | bytes 65568 | tf_op jit(solution)/shard_map/ppermute | solution.py:305
  24.6 2.8 %collective-permute-start.9 = (f32[2,128,128]{2,1,0:T(8,128)S(1)}, f32[2,128,128]{2,1,0:T(8,128)S(1)}, u32[]{:S(2)}, u32[]{:S(2)}) collective-permute-start(f32[2,128,128]{2,1,0:T(8,128)S(1)} %get-tuple-element.74), channel_id=1, source_target_pairs={{0,14},{1,7},{2,12},{3,5},{4,10},{5,3},{6,8},{7,1},{8,6},{9,15},{1... | collective-permute-start | bytes 393224 | tf_op jit(solution)/shard_map/ppermute | solution.py:310
  27.6 1.3 %collective-permute-start.11 = (f32[2,128,128]{2,1,0:T(8,128)S(1)}, f32[2,128,128]{2,1,0:T(8,128)S(1)}, u32[]{:S(2)}, u32[]{:S(2)}) collective-permute-start(f32[2,128,128]{2,1,0:T(8,128)S(1)} %get-tuple-element.76), channel_id=1, source_target_pairs={{0,4},{1,13},{2,6},{3,15},{4,0},{5,9},{6,2},{7,11},{8,12},{9,5},{1... | collective-permute-start | bytes 393224 | tf_op jit(solution)/shard_map/ppermute | solution.py:310
  28.9 0.7 %collective-permute-start.12 = (f32[128,128]{1,0:T(8,128)S(1)}, f32[128,128]{1,0:T(8,128)S(1)}, u32[]{:S(2)}, u32[]{:S(2)}) collective-permute-start(f32[128,128]{1,0:T(8,128)S(1)} %get-tuple-element.77), channel_id=1, source_target_pairs={{0,8},{1,9},{2,10},{3,11},{4,12},{5,13},{6,14},{7,15},{8,0},{9,1},... | collective-permute-start | bytes 196616 | tf_op jit(solution)/shard_map/ppermute | solution.py:310
  29.6 4.9 %collective-permute-done.12.refs_3_ = f32[128,128]{1,0:T(8,128)S(1)} collective-permute-done((f32[128,128]{1,0:T(8,128)S(1)}, f32[128,128]{1,0:T(8,128)S(1)}, u32[]{:S(2)}, u32[]{:S(2)}) %collective-permute-start.12) | collective-permute-done | bytes 65568 | tf_op jit(solution)/shard_map/ppermute | solution.py:310
  34.6 0.6 %collective-permute-start.13 = (f32[8,128,128]{2,1,0:T(8,128)S(1)}, f32[8,128,128]{2,1,0:T(8,128)S(1)}, u32[]{:S(2)}, u32[]{:S(2)}) collective-permute-start(f32[8,128,128]{2,1,0:T(8,128)S(1)} %shard_map.45), channel_id=1, source_target_pairs={{0,1},{1,0},{2,3},{3,2},{4,5},{5,4},{6,7},{7,6},{8,9},{9,8},{10,11... | collective-permute-start | bytes 1572872 | tf_op jit(solution)/shard_map/ppermute | solution.py:305
  35.2 0.4 %shard_map.46.d_ref = bf16[128,2048]{1,0:T(8,128)(2,1)S(1)} custom-call(bf16[128,2048]{1,0:T(8,128)(2,1)S(1)} %copy-done, f32[128,2048]{1,0:T(8,128)S(1)} %shard_map.40.l_ref, f32[8,128,128]{2,1,0:T(8,128)S(1)} %collective-permute-done.b_ref.g_ref, f32[2,128,128]{2,1,0:T(8,128)S(1)} %collective-permute-done.9.refs_0_, ...), custom_call_target="tpu_custom_call" | custom-call | flops 67108864 | bytes 2621440 | tf_op jit(solution)/shard_map/pallas_call | solution.py:18
  35.6 1.1 %collective-permute-done.13.c_ref = f32[8,128,128]{2,1,0:T(8,128)S(1)} collective-permute-done((f32[8,128,128]{2,1,0:T(8,128)S(1)}, f32[8,128,128]{2,1,0:T(8,128)S(1)}, u32[]{:S(2)}, u32[]{:S(2)}) %collective-permute-start.13) | collective-permute-done | bytes 524320 | tf_op jit(solution)/shard_map/ppermute | solution.py:305
  36.7 1.1 %shard_map.47 = (bf16[128,2048]{1,0:T(8,128)(2,1)}, bf16[128,2048]{1,0:T(8,128)(2,1)S(1)}) custom-call(bf16[128,2048]{1,0:T(8,128)(2,1)S(1)} %copy-done, f32[128,2048]{1,0:T(8,128)S(1)} %shard_map.40.l_ref, f32[8,128,128]{2,1,0:T(8,128)S(1)} %collective-permute-done.13.c_ref, bf16[128,2048]{1,0:T(8,128)(2,1)S(1)} %shard_map.46.d_ref), custom_call_target="tpu_custom_call", output_to_operand_aliasing={{1}: (3, {})} | custom-call | flops 67108864 | bytes 2621440 | tf_op jit(solution)/shard_map/pallas_call | solution.py:18
  (17 shorter events, 1.0 us)
Async XLA Ops:
  1.6 2.1 %collective-permute-start = (f32[8,128,128]{2,1,0:T(8,128)S(1)}, f32[8,128,128]{2,1,0:T(8,128)S(1)}, u32[]{:S(2)}, u32[]{:S(2)}) collective-permute-start(f32[8,128,128]{2,1,0:T(8,128)S(1)} %get-tuple-element.47), channel_id=1, source_target_pairs={{0,1},{1,0},{2,3},{3,2},{4,5},{5,4},{6,7},{7,6},{8,9},{9,8},{10,11... | collective-permute-start | bytes 1572872 | tf_op jit(solution)/shard_map/ppermute | solution.py:305
  2.4 7.4 %copy-start = (bf16[128,2048]{1,0:T(8,128)(2,1)S(1)}, bf16[128,2048]{1,0:T(8,128)(2,1)}, u32[]{:S(2)}) copy-start(bf16[128,2048]{1,0:T(8,128)(2,1)} %q_ref.4) | copy-start | bytes 1572868
  3.7 11.1 %collective-permute-start.1 = (f32[2,128,128]{2,1,0:T(8,128)S(1)}, f32[2,128,128]{2,1,0:T(8,128)S(1)}, u32[]{:S(2)}, u32[]{:S(2)}) collective-permute-start(f32[2,128,128]{2,1,0:T(8,128)S(1)} %get-tuple-element.48), channel_id=1, source_target_pairs={{0,14},{1,7},{2,12},{3,5},{4,10},{5,3},{6,8},{7,1},{8,6},{9,15},{1... | collective-permute-start | bytes 393224 | tf_op jit(solution)/shard_map/ppermute | solution.py:310
  8.6 6.2 %collective-permute-start.2 = (f32[2,128,128]{2,1,0:T(8,128)S(1)}, f32[2,128,128]{2,1,0:T(8,128)S(1)}, u32[]{:S(2)}, u32[]{:S(2)}) collective-permute-start(f32[2,128,128]{2,1,0:T(8,128)S(1)} %get-tuple-element.49), channel_id=1, source_target_pairs={{0,2},{1,11},{2,0},{3,9},{4,6},{5,15},{6,4},{7,13},{8,10},{9,3},{1... | collective-permute-start | bytes 393224 | tf_op jit(solution)/shard_map/ppermute | solution.py:310
  9.1 6.2 %collective-permute-start.3 = (f32[2,128,128]{2,1,0:T(8,128)S(1)}, f32[2,128,128]{2,1,0:T(8,128)S(1)}, u32[]{:S(2)}, u32[]{:S(2)}) collective-permute-start(f32[2,128,128]{2,1,0:T(8,128)S(1)} %get-tuple-element.50), channel_id=1, source_target_pairs={{0,4},{1,13},{2,6},{3,15},{4,0},{5,9},{6,2},{7,11},{8,12},{9,5},{1... | collective-permute-start | bytes 393224 | tf_op jit(solution)/shard_map/ppermute | solution.py:310
  9.6 5.1 %collective-permute-start.4 = (f32[128,128]{1,0:T(8,128)S(1)}, f32[128,128]{1,0:T(8,128)S(1)}, u32[]{:S(2)}, u32[]{:S(2)}) collective-permute-start(f32[128,128]{1,0:T(8,128)S(1)} %get-tuple-element.51), channel_id=1, source_target_pairs={{0,8},{1,9},{2,10},{3,11},{4,12},{5,13},{6,14},{7,15},{8,0},{9,1},... | collective-permute-start | bytes 196616 | tf_op jit(solution)/shard_map/ppermute | solution.py:310
  15.3 1.5 %collective-permute-start.5 = (f32[3,128,128]{2,1,0:T(8,128)S(1)}, f32[3,128,128]{2,1,0:T(8,128)S(1)}, u32[]{:S(2)}, u32[]{:S(2)}) collective-permute-start(f32[3,128,128]{2,1,0:T(8,128)S(1)} %shard_map.41), channel_id=1, source_target_pairs={{0,1},{1,0},{2,3},{3,2},{4,5},{5,4},{6,7},{7,6},{8,9},{9,8},{10,11... | collective-permute-start | bytes 589832 | tf_op jit(solution)/shard_map/ppermute | solution.py:305
  16.8 5.3 %collective-permute-start.7 = (f32[5,128,128]{2,1,0:T(8,128)S(1)}, f32[5,128,128]{2,1,0:T(8,128)S(1)}, u32[]{:S(2)}, u32[]{:S(2)}) collective-permute-start(f32[5,128,128]{2,1,0:T(8,128)S(1)} %get-tuple-element.60), channel_id=1, source_target_pairs={{0,1},{1,0},{2,3},{3,2},{4,5},{5,4},{6,7},{7,6},{8,9},{9,8},{10,11... | collective-permute-start | bytes 983048 | tf_op jit(solution)/shard_map/ppermute | solution.py:305
  17.1 5.0 %collective-permute-start.6 = (f32[128,128]{1,0:T(8,128)S(1)}, f32[128,128]{1,0:T(8,128)S(1)}, u32[]{:S(2)}, u32[]{:S(2)}) collective-permute-start(f32[128,128]{1,0:T(8,128)S(1)} %get-tuple-element.59), channel_id=1, source_target_pairs={{0,17},{1,16},{2,19},{3,18},{4,21},{5,20},{6,23},{7,22},{8,25},{9,... | collective-permute-start | bytes 196616 | tf_op jit(solution)/shard_map/ppermute | solution.py:340
  22.1 2.5 %collective-permute-start.8 = (f32[128,128]{1,0:T(8,128)S(1)}, f32[128,128]{1,0:T(8,128)S(1)}, u32[]{:S(2)}, u32[]{:S(2)}) collective-permute-start(f32[128,128]{1,0:T(8,128)S(1)} %collective-permute-done.6.o_ref), channel_id=1, source_target_pairs={{0,1},{1,0},{2,3},{3,2},{4,5},{5,4},{6,7},{7,6},{8,9},{9,8},{10,11... | collective-permute-start | bytes 196616 | tf_op jit(solution)/shard_map/ppermute | solution.py:305
  24.6 9.9 %collective-permute-start.9 = (f32[2,128,128]{2,1,0:T(8,128)S(1)}, f32[2,128,128]{2,1,0:T(8,128)S(1)}, u32[]{:S(2)}, u32[]{:S(2)}) collective-permute-start(f32[2,128,128]{2,1,0:T(8,128)S(1)} %get-tuple-element.74), channel_id=1, source_target_pairs={{0,14},{1,7},{2,12},{3,5},{4,10},{5,3},{6,8},{7,1},{8,6},{9,15},{1... | collective-permute-start | bytes 393224 | tf_op jit(solution)/shard_map/ppermute | solution.py:310
  27.4 7.1 %collective-permute-start.10 = (f32[2,128,128]{2,1,0:T(8,128)S(1)}, f32[2,128,128]{2,1,0:T(8,128)S(1)}, u32[]{:S(2)}, u32[]{:S(2)}) collective-permute-start(f32[2,128,128]{2,1,0:T(8,128)S(1)} %get-tuple-element.75), channel_id=1, source_target_pairs={{0,2},{1,11},{2,0},{3,9},{4,6},{5,15},{6,4},{7,13},{8,10},{9,3},{1... | collective-permute-start | bytes 393224 | tf_op jit(solution)/shard_map/ppermute | solution.py:310
  27.6 6.9 %collective-permute-start.11 = (f32[2,128,128]{2,1,0:T(8,128)S(1)}, f32[2,128,128]{2,1,0:T(8,128)S(1)}, u32[]{:S(2)}, u32[]{:S(2)}) collective-permute-start(f32[2,128,128]{2,1,0:T(8,128)S(1)} %get-tuple-element.76), channel_id=1, source_target_pairs={{0,4},{1,13},{2,6},{3,15},{4,0},{5,9},{6,2},{7,11},{8,12},{9,5},{1... | collective-permute-start | bytes 393224 | tf_op jit(solution)/shard_map/ppermute | solution.py:310
  28.9 5.6 %collective-permute-start.12 = (f32[128,128]{1,0:T(8,128)S(1)}, f32[128,128]{1,0:T(8,128)S(1)}, u32[]{:S(2)}, u32[]{:S(2)}) collective-permute-start(f32[128,128]{1,0:T(8,128)S(1)} %get-tuple-element.77), channel_id=1, source_target_pairs={{0,8},{1,9},{2,10},{3,11},{4,12},{5,13},{6,14},{7,15},{8,0},{9,1},... | collective-permute-start | bytes 196616 | tf_op jit(solution)/shard_map/ppermute | solution.py:310
  34.6 2.1 %collective-permute-start.13 = (f32[8,128,128]{2,1,0:T(8,128)S(1)}, f32[8,128,128]{2,1,0:T(8,128)S(1)}, u32[]{:S(2)}, u32[]{:S(2)}) collective-permute-start(f32[8,128,128]{2,1,0:T(8,128)S(1)} %shard_map.45), channel_id=1, source_target_pairs={{0,1},{1,0},{2,3},{3,2},{4,5},{5,4},{6,7},{7,6},{8,9},{9,8},{10,11... | collective-permute-start | bytes 1572872 | tf_op jit(solution)/shard_map/ppermute | solution.py:305

commit v7 on v6

--- a/solution.py
+++ b/solution.py
@@ -326,12 +326,12 @@
     got = swap_cores(given)
     kept = kept_states(keys, values, group)
     *pairs, near, mine = chip_pieces(kept, got)
-    later_q, _ = lax.optimization_barrier((queries, mine))
     pairs, near = pairings(pairs, near, chips, cores, group)
-    local = local_part(later_q, keys, values)
-    *pairs, near, local = lax.optimization_barrier((*pairs, near, local))
+    *pairs, near = lax.optimization_barrier((*pairs, near))
     swapped = swap_cores(for_other_core(pairs))
     running, lacking = gathered(pairs, swapped, near, mine)
+    later_q, _ = lax.optimization_barrier((queries, running))
+    local = local_part(later_q, keys, values)
     cube = lax.axis_index("wide") // group
     earlier = jnp.zeros_like(running) if groups != 2 else None
     crossed = 1 if groups == 2 else 0
@@ -346,7 +346,7 @@
         running = running + seen
         step *= 2
     received = swap_cores(lacking)
-    earlier, received = lax.optimization_barrier((earlier, received))
+    earlier, received, local = lax.optimization_barrier((earlier, received, local))
     others = swap_cores(earlier)
     if crossed:
         earlier, others = others, earlier

time: 38 us -> 38 us (level)
    ppermute x8, waiting for transfers between devices: 7.78 us -> 10.4 us  [pair_chips(): return lax.ppermute(block, ('wide', 'narrow'), route)]
    ppermute x1, waiting for transfers between devices: 2.31 us -> 0.01 us  [shards(): lax.ppermute(running, ('wide', 'narrow'), [(i * cores + c, (i ^ step * gr...]
  transfers between devices with their start and end apart: 14 -> 14, of which waited for: 8 -> 7; matrix products, arithmetic and copies ran while one was open for 0% -> 0% of each run, Pallas kernels for 9% -> 9%
where the time goes in v7:
time: 38 us; the launch traced here: 37.9 us
  starting transfers between devices  16.8 us (44%)
  waiting for transfers between devices  14.7 us (39%)
  Pallas kernels  6.32 us (17%)
    ppermute x8, starting transfers between devices, pair_chips(): return lax.ppermute(block, ('wide', 'narrow'), route)  11.1 us
    ppermute x8, waiting for transfers between devices, pair_chips(): return lax.ppermute(block, ('wide', 'narrow'), route)  10.4 us
    pallas_call x11, Pallas kernels, call(): pl.pallas_call(kernel, out_shape=outs, in_specs=ins or [VMEM] * len(args)...  6.32 us
    ppermute x5, waiting for transfers between devices, swap_cores(): return lax.ppermute(block, 'narrow', [(0, 1), (1, 0)])  4.35 us
    ppermute x5, starting transfers between devices, swap_cores(): return lax.ppermute(block, 'narrow', [(0, 1), (1, 0)])  2.96 us
    ppermute x1, starting transfers between devices, shards(): lax.ppermute(running, ('wide', 'narrow'), [(i * cores + c, (i ^ step * gr...  2.68 us
  transfers between devices with their start and end apart: 14, of which 7 were waited for; matrix products, arithmetic and copies ran while one was open for 0% of the time, Pallas kernels for 9%

profile of v7, /device:TPU:0, one launch (start us, length us, event | category | flops | bytes accessed | tf_op | source)
XLA Modules:
  0.0 37.9 jit_solution(13012822063878383094)
XLA Ops:
  0.0 1.5 %shard_map.37 = (f32[8,128,128]{2,1,0:T(8,128)S(1)}, bf16[128,2048]{1,0:T(8,128)(2,1)S(1)}, bf16[128,2048]{1,0:T(8,128)(2,1)S(1)}) custom-call(bf16[128,2048]{1,0:T(8,128)(2,1)} %k_hbm.1, bf16[128,2048]{1,0:T(8,128)(2,1)} %v_hbm.1), custom_call_target="tpu_custom_call" | custom-call | flops 33554432 | bytes 1048576 | tf_op jit(solution)/shard_map/pallas_call | solution.py:18
  1.6 0.5 %collective-permute-start = (f32[8,128,128]{2,1,0:T(8,128)S(1)}, f32[8,128,128]{2,1,0:T(8,128)S(1)}, u32[]{:S(2)}, u32[]{:S(2)}) collective-permute-start(f32[8,128,128]{2,1,0:T(8,128)S(1)} %get-tuple-element.47), channel_id=1, source_target_pairs={{0,1},{1,0},{2,3},{3,2},{4,5},{5,4},{6,7},{7,6},{8,9},{9,8},{10,11... | collective-permute-start | bytes 1572872 | tf_op jit(solution)/shard_map/ppermute | solution.py:305
  2.1 0.3 shard_map.38.a_ref.k_ref
  2.4 1.3 %collective-permute-done.b_ref.g_ref = f32[8,128,128]{2,1,0:T(8,128)S(1)} collective-permute-done((f32[8,128,128]{2,1,0:T(8,128)S(1)}, f32[8,128,128]{2,1,0:T(8,128)S(1)}, u32[]{:S(2)}, u32[]{:S(2)}) %collective-permute-start) | collective-permute-done | bytes 524320 | tf_op jit(solution)/shard_map/ppermute | solution.py:305
  3.7 4.9 %collective-permute-start.1 = (f32[2,128,128]{2,1,0:T(8,128)S(1)}, f32[2,128,128]{2,1,0:T(8,128)S(1)}, u32[]{:S(2)}, u32[]{:S(2)}) collective-permute-start(f32[2,128,128]{2,1,0:T(8,128)S(1)} %get-tuple-element.48), channel_id=1, source_target_pairs={{0,14},{1,7},{2,12},{3,5},{4,10},{5,3},{6,8},{7,1},{8,6},{9,15},{1... | collective-permute-start | bytes 393224 | tf_op jit(solution)/shard_map/ppermute | solution.py:310
  8.6 0.5 %collective-permute-start.2 = (f32[2,128,128]{2,1,0:T(8,128)S(1)}, f32[2,128,128]{2,1,0:T(8,128)S(1)}, u32[]{:S(2)}, u32[]{:S(2)}) collective-permute-start(f32[2,128,128]{2,1,0:T(8,128)S(1)} %get-tuple-element.49), channel_id=1, source_target_pairs={{0,2},{1,11},{2,0},{3,9},{4,6},{5,15},{6,4},{7,13},{8,10},{9,3},{1... | collective-permute-start | bytes 393224 | tf_op jit(solution)/shard_map/ppermute | solution.py:310
  9.1 0.5 %collective-permute-start.3 = (f32[2,128,128]{2,1,0:T(8,128)S(1)}, f32[2,128,128]{2,1,0:T(8,128)S(1)}, u32[]{:S(2)}, u32[]{:S(2)}) collective-permute-start(f32[2,128,128]{2,1,0:T(8,128)S(1)} %get-tuple-element.50), channel_id=1, source_target_pairs={{0,4},{1,13},{2,6},{3,15},{4,0},{5,9},{6,2},{7,11},{8,12},{9,5},{1... | collective-permute-start | bytes 393224 | tf_op jit(solution)/shard_map/ppermute | solution.py:310
  9.8 5.0 %collective-permute-done.4.refs_4_ = f32[128,128]{1,0:T(8,128)S(1)} collective-permute-done((f32[128,128]{1,0:T(8,128)S(1)}, f32[128,128]{1,0:T(8,128)S(1)}, u32[]{:S(2)}, u32[]{:S(2)}) %collective-permute-start.4) | collective-permute-done | bytes 65568 | tf_op jit(solution)/shard_map/ppermute | solution.py:310
  14.8 0.5 %collective-permute-done.3.refs_2_ = f32[2,128,128]{2,1,0:T(8,128)S(1)} collective-permute-done((f32[2,128,128]{2,1,0:T(8,128)S(1)}, f32[2,128,128]{2,1,0:T(8,128)S(1)}, u32[]{:S(2)}, u32[]{:S(2)}) %collective-permute-start.3) | collective-permute-done | bytes 131104 | tf_op jit(solution)/shard_map/ppermute | solution.py:310
  15.3 0.3 collective-permute-start.5
  15.6 1.2 %collective-permute-done.5.refs_3_ = f32[3,128,128]{2,1,0:T(8,128)S(1)} collective-permute-done((f32[3,128,128]{2,1,0:T(8,128)S(1)}, f32[3,128,128]{2,1,0:T(8,128)S(1)}, u32[]{:S(2)}, u32[]{:S(2)}) %collective-permute-start.5) | collective-permute-done | bytes 196640 | tf_op jit(solution)/shard_map/ppermute | solution.py:305
  16.8 0.3 collective-permute-start.7
  17.1 2.7 %collective-permute-start.6 = (f32[128,128]{1,0:T(8,128)S(1)}, f32[128,128]{1,0:T(8,128)S(1)}, u32[]{:S(2)}, u32[]{:S(2)}) collective-permute-start(f32[128,128]{1,0:T(8,128)S(1)} %get-tuple-element.57), channel_id=1, source_target_pairs={{0,17},{1,16},{2,19},{3,18},{4,21},{5,20},{6,23},{7,22},{8,25},{9,... | collective-permute-start | bytes 196616 | tf_op jit(solution)/shard_map/ppermute | solution.py:340
  19.8 2.6 %shard_map.42.l_ref = f32[128,2048]{1,0:T(8,128)S(1)} custom-call(bf16[128,2048]{1,0:T(8,128)(2,1)S(1)} %copy-done, bf16[128,2048]{1,0:T(8,128)(2,1)S(1)} %get-tuple-element.45.k_ref, bf16[128,2048]{1,0:T(8,128)(2,1)S(1)} %get-tuple-element.46.v_ref), custom_call_target="tpu_custom_call" | custom-call | flops 134217728 | bytes 1572864 | tf_op jit(solution)/shard_map/pallas_call | solution.py:18
  22.4 1.3 %collective-permute-start.8 = (f32[128,128]{1,0:T(8,128)S(1)}, f32[128,128]{1,0:T(8,128)S(1)}, u32[]{:S(2)}, u32[]{:S(2)}) collective-permute-start(f32[128,128]{1,0:T(8,128)S(1)} %collective-permute-done.6.o_ref), channel_id=1, source_target_pairs={{0,1},{1,0},{2,3},{3,2},{4,5},{5,4},{6,7},{7,6},{8,9},{9,8},{10,11... | collective-permute-start | bytes 196616 | tf_op jit(solution)/shard_map/ppermute | solution.py:305
  23.8 0.8 %collective-permute-done.8.e_ref = f32[128,128]{1,0:T(8,128)S(1)} collective-permute-done((f32[128,128]{1,0:T(8,128)S(1)}, f32[128,128]{1,0:T(8,128)S(1)}, u32[]{:S(2)}, u32[]{:S(2)}) %collective-permute-start.8) | collective-permute-done | bytes 65568 | tf_op jit(solution)/shard_map/ppermute | solution.py:305
  24.6 2.8 %collective-permute-start.9 = (f32[2,128,128]{2,1,0:T(8,128)S(1)}, f32[2,128,128]{2,1,0:T(8,128)S(1)}, u32[]{:S(2)}, u32[]{:S(2)}) collective-permute-start(f32[2,128,128]{2,1,0:T(8,128)S(1)} %get-tuple-element.74), channel_id=1, source_target_pairs={{0,14},{1,7},{2,12},{3,5},{4,10},{5,3},{6,8},{7,1},{8,6},{9,15},{1... | collective-permute-start | bytes 393224 | tf_op jit(solution)/shard_map/ppermute | solution.py:310
  27.6 1.3 %collective-permute-start.11 = (f32[2,128,128]{2,1,0:T(8,128)S(1)}, f32[2,128,128]{2,1,0:T(8,128)S(1)}, u32[]{:S(2)}, u32[]{:S(2)}) collective-permute-start(f32[2,128,128]{2,1,0:T(8,128)S(1)} %get-tuple-element.76), channel_id=1, source_target_pairs={{0,4},{1,13},{2,6},{3,15},{4,0},{5,9},{6,2},{7,11},{8,12},{9,5},{1... | collective-permute-start | bytes 393224 | tf_op jit(solution)/shard_map/ppermute | solution.py:310
  28.9 0.7 %collective-permute-start.12 = (f32[128,128]{1,0:T(8,128)S(1)}, f32[128,128]{1,0:T(8,128)S(1)}, u32[]{:S(2)}, u32[]{:S(2)}) collective-permute-start(f32[128,128]{1,0:T(8,128)S(1)} %get-tuple-element.77), channel_id=1, source_target_pairs={{0,8},{1,9},{2,10},{3,11},{4,12},{5,13},{6,14},{7,15},{8,0},{9,1},... | collective-permute-start | bytes 196616 | tf_op jit(solution)/shard_map/ppermute | solution.py:310
  29.6 4.9 %collective-permute-done.12.refs_3_ = f32[128,128]{1,0:T(8,128)S(1)} collective-permute-done((f32[128,128]{1,0:T(8,128)S(1)}, f32[128,128]{1,0:T(8,128)S(1)}, u32[]{:S(2)}, u32[]{:S(2)}) %collective-permute-start.12) | collective-permute-done | bytes 65568 | tf_op jit(solution)/shard_map/ppermute | solution.py:310
  34.6 0.6 %collective-permute-start.13 = (f32[8,128,128]{2,1,0:T(8,128)S(1)}, f32[8,128,128]{2,1,0:T(8,128)S(1)}, u32[]{:S(2)}, u32[]{:S(2)}) collective-permute-start(f32[8,128,128]{2,1,0:T(8,128)S(1)} %shard_map.45), channel_id=1, source_target_pairs={{0,1},{1,0},{2,3},{3,2},{4,5},{5,4},{6,7},{7,6},{8,9},{9,8},{10,11... | collective-permute-start | bytes 1572872 | tf_op jit(solution)/shard_map/ppermute | solution.py:305
  35.2 0.4 %shard_map.46.d_ref = bf16[128,2048]{1,0:T(8,128)(2,1)S(1)} custom-call(bf16[128,2048]{1,0:T(8,128)(2,1)S(1)} %copy-done, f32[128,2048]{1,0:T(8,128)S(1)} %shard_map.42.l_ref, f32[8,128,128]{2,1,0:T(8,128)S(1)} %collective-permute-done.b_ref.g_ref, f32[2,128,128]{2,1,0:T(8,128)S(1)} %collective-permute-done.9.refs_0_, ...), custom_call_target="tpu_custom_call" | custom-call | flops 67108864 | bytes 2621440 | tf_op jit(solution)/shard_map/pallas_call | solution.py:18
  35.6 1.1 %collective-permute-done.13.c_ref = f32[8,128,128]{2,1,0:T(8,128)S(1)} collective-permute-done((f32[8,128,128]{2,1,0:T(8,128)S(1)}, f32[8,128,128]{2,1,0:T(8,128)S(1)}, u32[]{:S(2)}, u32[]{:S(2)}) %collective-permute-start.13) | collective-permute-done | bytes 524320 | tf_op jit(solution)/shard_map/ppermute | solution.py:305
  36.7 1.1 %shard_map.47 = (bf16[128,2048]{1,0:T(8,128)(2,1)}, bf16[128,2048]{1,0:T(8,128)(2,1)S(1)}) custom-call(bf16[128,2048]{1,0:T(8,128)(2,1)S(1)} %copy-done, f32[128,2048]{1,0:T(8,128)S(1)} %shard_map.42.l_ref, f32[8,128,128]{2,1,0:T(8,128)S(1)} %collective-permute-done.13.c_ref, bf16[128,2048]{1,0:T(8,128)(2,1)S(1)} %shard_map.46.d_ref), custom_call_target="tpu_custom_call", output_to_operand_aliasing={{1}: (3, {})} | custom-call | flops 67108864 | bytes 2621440 | tf_op jit(solution)/shard_map/pallas_call | solution.py:18
  (17 shorter events, 0.8 us)
Async XLA Ops:
  1.6 2.1 %collective-permute-start = (f32[8,128,128]{2,1,0:T(8,128)S(1)}, f32[8,128,128]{2,1,0:T(8,128)S(1)}, u32[]{:S(2)}, u32[]{:S(2)}) collective-permute-start(f32[8,128,128]{2,1,0:T(8,128)S(1)} %get-tuple-element.47), channel_id=1, source_target_pairs={{0,1},{1,0},{2,3},{3,2},{4,5},{5,4},{6,7},{7,6},{8,9},{9,8},{10,11... | collective-permute-start | bytes 1572872 | tf_op jit(solution)/shard_map/ppermute | solution.py:305
  3.7 11.1 %collective-permute-start.1 = (f32[2,128,128]{2,1,0:T(8,128)S(1)}, f32[2,128,128]{2,1,0:T(8,128)S(1)}, u32[]{:S(2)}, u32[]{:S(2)}) collective-permute-start(f32[2,128,128]{2,1,0:T(8,128)S(1)} %get-tuple-element.48), channel_id=1, source_target_pairs={{0,14},{1,7},{2,12},{3,5},{4,10},{5,3},{6,8},{7,1},{8,6},{9,15},{1... | collective-permute-start | bytes 393224 | tf_op jit(solution)/shard_map/ppermute | solution.py:310
  8.6 6.2 %collective-permute-start.2 = (f32[2,128,128]{2,1,0:T(8,128)S(1)}, f32[2,128,128]{2,1,0:T(8,128)S(1)}, u32[]{:S(2)}, u32[]{:S(2)}) collective-permute-start(f32[2,128,128]{2,1,0:T(8,128)S(1)} %get-tuple-element.49), channel_id=1, source_target_pairs={{0,2},{1,11},{2,0},{3,9},{4,6},{5,15},{6,4},{7,13},{8,10},{9,3},{1... | collective-permute-start | bytes 393224 | tf_op jit(solution)/shard_map/ppermute | solution.py:310
  9.1 6.2 %collective-permute-start.3 = (f32[2,128,128]{2,1,0:T(8,128)S(1)}, f32[2,128,128]{2,1,0:T(8,128)S(1)}, u32[]{:S(2)}, u32[]{:S(2)}) collective-permute-start(f32[2,128,128]{2,1,0:T(8,128)S(1)} %get-tuple-element.50), channel_id=1, source_target_pairs={{0,4},{1,13},{2,6},{3,15},{4,0},{5,9},{6,2},{7,11},{8,12},{9,5},{1... | collective-permute-start | bytes 393224 | tf_op jit(solution)/shard_map/ppermute | solution.py:310
  9.6 10.2 %copy-start = (bf16[128,2048]{1,0:T(8,128)(2,1)S(1)}, bf16[128,2048]{1,0:T(8,128)(2,1)}, u32[]{:S(2)}) copy-start(bf16[128,2048]{1,0:T(8,128)(2,1)} %q_ref.4) | copy-start | bytes 1572868
  9.6 5.1 %collective-permute-start.4 = (f32[128,128]{1,0:T(8,128)S(1)}, f32[128,128]{1,0:T(8,128)S(1)}, u32[]{:S(2)}, u32[]{:S(2)}) collective-permute-start(f32[128,128]{1,0:T(8,128)S(1)} %get-tuple-element.51), channel_id=1, source_target_pairs={{0,8},{1,9},{2,10},{3,11},{4,12},{5,13},{6,14},{7,15},{8,0},{9,1},... | collective-permute-start | bytes 196616 | tf_op jit(solution)/shard_map/ppermute | solution.py:310
  15.3 1.5 %collective-permute-start.5 = (f32[3,128,128]{2,1,0:T(8,128)S(1)}, f32[3,128,128]{2,1,0:T(8,128)S(1)}, u32[]{:S(2)}, u32[]{:S(2)}) collective-permute-start(f32[3,128,128]{2,1,0:T(8,128)S(1)} %shard_map.40), channel_id=1, source_target_pairs={{0,1},{1,0},{2,3},{3,2},{4,5},{5,4},{6,7},{7,6},{8,9},{9,8},{10,11... | collective-permute-start | bytes 589832 | tf_op jit(solution)/shard_map/ppermute | solution.py:305
  16.8 5.6 %collective-permute-start.7 = (f32[5,128,128]{2,1,0:T(8,128)S(1)}, f32[5,128,128]{2,1,0:T(8,128)S(1)}, u32[]{:S(2)}, u32[]{:S(2)}) collective-permute-start(f32[5,128,128]{2,1,0:T(8,128)S(1)} %get-tuple-element.58), channel_id=1, source_target_pairs={{0,1},{1,0},{2,3},{3,2},{4,5},{5,4},{6,7},{7,6},{8,9},{9,8},{10,11... | collective-permute-start | bytes 983048 | tf_op jit(solution)/shard_map/ppermute | solution.py:305
  17.1 5.3 %collective-permute-start.6 = (f32[128,128]{1,0:T(8,128)S(1)}, f32[128,128]{1,0:T(8,128)S(1)}, u32[]{:S(2)}, u32[]{:S(2)}) collective-permute-start(f32[128,128]{1,0:T(8,128)S(1)} %get-tuple-element.57), channel_id=1, source_target_pairs={{0,17},{1,16},{2,19},{3,18},{4,21},{5,20},{6,23},{7,22},{8,25},{9,... | collective-permute-start | bytes 196616 | tf_op jit(solution)/shard_map/ppermute | solution.py:340
  22.4 2.2 %collective-permute-start.8 = (f32[128,128]{1,0:T(8,128)S(1)}, f32[128,128]{1,0:T(8,128)S(1)}, u32[]{:S(2)}, u32[]{:S(2)}) collective-permute-start(f32[128,128]{1,0:T(8,128)S(1)} %collective-permute-done.6.o_ref), channel_id=1, source_target_pairs={{0,1},{1,0},{2,3},{3,2},{4,5},{5,4},{6,7},{7,6},{8,9},{9,8},{10,11... | collective-permute-start | bytes 196616 | tf_op jit(solution)/shard_map/ppermute | solution.py:305
  24.6 9.9 %collective-permute-start.9 = (f32[2,128,128]{2,1,0:T(8,128)S(1)}, f32[2,128,128]{2,1,0:T(8,128)S(1)}, u32[]{:S(2)}, u32[]{:S(2)}) collective-permute-start(f32[2,128,128]{2,1,0:T(8,128)S(1)} %get-tuple-element.74), channel_id=1, source_target_pairs={{0,14},{1,7},{2,12},{3,5},{4,10},{5,3},{6,8},{7,1},{8,6},{9,15},{1... | collective-permute-start | bytes 393224 | tf_op jit(solution)/shard_map/ppermute | solution.py:310
  27.4 7.1 %collective-permute-start.10 = (f32[2,128,128]{2,1,0:T(8,128)S(1)}, f32[2,128,128]{2,1,0:T(8,128)S(1)}, u32[]{:S(2)}, u32[]{:S(2)}) collective-permute-start(f32[2,128,128]{2,1,0:T(8,128)S(1)} %get-tuple-element.75), channel_id=1, source_target_pairs={{0,2},{1,11},{2,0},{3,9},{4,6},{5,15},{6,4},{7,13},{8,10},{9,3},{1... | collective-permute-start | bytes 393224 | tf_op jit(solution)/shard_map/ppermute | solution.py:310
  27.6 6.9 %collective-permute-start.11 = (f32[2,128,128]{2,1,0:T(8,128)S(1)}, f32[2,128,128]{2,1,0:T(8,128)S(1)}, u32[]{:S(2)}, u32[]{:S(2)}) collective-permute-start(f32[2,128,128]{2,1,0:T(8,128)S(1)} %get-tuple-element.76), channel_id=1, source_target_pairs={{0,4},{1,13},{2,6},{3,15},{4,0},{5,9},{6,2},{7,11},{8,12},{9,5},{1... | collective-permute-start | bytes 393224 | tf_op jit(solution)/shard_map/ppermute | solution.py:310
  28.9 5.6 %collective-permute-start.12 = (f32[128,128]{1,0:T(8,128)S(1)}, f32[128,128]{1,0:T(8,128)S(1)}, u32[]{:S(2)}, u32[]{:S(2)}) collective-permute-start(f32[128,128]{1,0:T(8,128)S(1)} %get-tuple-element.77), channel_id=1, source_target_pairs={{0,8},{1,9},{2,10},{3,11},{4,12},{5,13},{6,14},{7,15},{8,0},{9,1},... | collective-permute-start | bytes 196616 | tf_op jit(solution)/shard_map/ppermute | solution.py:310
  34.6 2.1 %collective-permute-start.13 = (f32[8,128,128]{2,1,0:T(8,128)S(1)}, f32[8,128,128]{2,1,0:T(8,128)S(1)}, u32[]{:S(2)}, u32[]{:S(2)}) collective-permute-start(f32[8,128,128]{2,1,0:T(8,128)S(1)} %shard_map.45), channel_id=1, source_target_pairs={{0,1},{1,0},{2,3},{3,2},{4,5},{5,4},{6,7},{7,6},{8,9},{9,8},{10,11... | collective-permute-start | bytes 1572872 | tf_op jit(solution)/shard_map/ppermute | solution.py:305
